TPU v7x, 512 devices: a whole 4x4x16 slice. The times are simulated.
512 devices in a mesh: ctx: 64 (over y_hi, z, core), ch: 8 (over x, y_lo).
Axes of the slice: x: 4, y: 4 (y_hi: 2, y_lo: 2; y = y_hi * 2 + y_lo), z: 16, core: 2. Of those that a mesh axis runs over, the one named last changes fastest.
Arguments:
- tokens: bfloat16 [8192, 8192], P('ctx', 'ch'), may hold values from -6 to 6
- weights: bfloat16 [3, 8192, 512], P(None, 'ch'), may hold values from -0.0625 to 0.0625
- filter_taps: float32 [64, 8, 8192], P('ctx', 'ch'), may hold values from -32 to 32
- cotangent: bfloat16 [512, 8192], P('ch', 'ctx'), may hold values from -6 to 6
Outputs:
- gated_out: bfloat16 [512, 8192], P('ch', 'ctx')
- input_grad: bfloat16 [8192, 8192], P('ctx', 'ch')
- filter_grad: float32 [64, 8, 8192], P('ctx', 'ch')
All inputs are finite; a program needn't handle non-finite values.
Results may differ from a plain program's by a relative error of at most 0.03.
Values may be sent and summed in bfloat16 or wider, within the bound.
No kernel may reach another device: no remote copies, remote signals or barrier semaphores. Data moves between devices by JAX's collectives and lax.ppermute only.
A program may use at most 64 MiB of HBM per device.

v0:
```python
import math

import jax
import jax.numpy as jnp
from jax import lax
from jax.sharding import PartitionSpec as P

highest_precision = lax.Precision.HIGHEST


def dft_tables(table_size):
    row_index = lax.broadcasted_iota(jnp.int32, (table_size, table_size), 0)
    col_index = lax.broadcasted_iota(jnp.int32, (table_size, table_size), 1)
    angles = (row_index * col_index % table_size).astype(jnp.float32) * (2.0 * math.pi / table_size)
    return (jnp.cos(angles), jnp.sin(angles))


def twiddle_tables(outer_size, inner_size):
    total_len = outer_size * inner_size
    row_index = lax.broadcasted_iota(jnp.int32, (outer_size, inner_size), 0)
    col_index = lax.broadcasted_iota(jnp.int32, (outer_size, inner_size), 1)
    angles = (row_index * col_index % total_len).astype(jnp.float32) * (2.0 * math.pi / total_len)
    return (jnp.cos(angles), jnp.sin(angles))


def split_sizes(total_len):
    binary_digits = total_len.bit_length() - 1
    outer_size = 2 ** ((binary_digits + 1) // 2)
    return (outer_size, total_len // outer_size)


def contract(form, left_side, right_side):
    return jnp.einsum(form, left_side, right_side, precision=highest_precision)


def transform(signal):
    planes, total_len = signal.shape
    outer_size, inner_size = split_sizes(total_len)
    cos_outer, sin_outer = dft_tables(outer_size)
    cos_inner, sin_inner = dft_tables(inner_size)
    twid_cos, twid_sin = twiddle_tables(outer_size, inner_size)
    folded = signal.reshape(planes, outer_size, inner_size)
    first_re = contract("pba,bk->pka", folded, cos_outer)
    first_im = -contract("pba,bk->pka", folded, sin_outer)
    turned_re = first_re * twid_cos + first_im * twid_sin
    turned_im = first_im * twid_cos - first_re * twid_sin
    out_re = contract("pka,aj->pkj", turned_re, cos_inner) + contract(
        "pka,aj->pkj", turned_im, sin_inner
    )
    out_im = contract("pka,aj->pkj", turned_im, cos_inner) - contract(
        "pka,aj->pkj", turned_re, sin_inner
    )
    return (out_re, out_im)


def inverse(spec_re, spec_im):
    planes, outer_size, inner_size = spec_re.shape
    cos_outer, sin_outer = dft_tables(outer_size)
    cos_inner, sin_inner = dft_tables(inner_size)
    twid_cos, twid_sin = twiddle_tables(outer_size, inner_size)
    mid_re = contract("pkj,aj->pka", spec_re, cos_inner) - contract(
        "pkj,aj->pka", spec_im, sin_inner
    )
    mid_im = contract("pkj,aj->pka", spec_im, cos_inner) + contract(
        "pkj,aj->pka", spec_re, sin_inner
    )
    turned_re = mid_re * twid_cos - mid_im * twid_sin
    turned_im = mid_im * twid_cos + mid_re * twid_sin
    result = contract("pka,bk->pba", turned_re, cos_outer) - contract(
        "pka,bk->pba", turned_im, sin_outer
    )
    return result.reshape(planes, outer_size * inner_size) * (1.0 / (outer_size * inner_size))


def spectrum(signal):
    padded = jnp.concatenate([signal, jnp.zeros_like(signal)], axis=1)
    return transform(padded)


def complex_times(left_pair, right_pair):
    return (
        left_pair[0] * right_pair[0] - left_pair[1] * right_pair[1],
        left_pair[0] * right_pair[1] + left_pair[1] * right_pair[0],
    )


def complex_conj_times(left_pair, right_pair):
    return (
        left_pair[0] * right_pair[0] + left_pair[1] * right_pair[1],
        left_pair[1] * right_pair[0] - left_pair[0] * right_pair[1],
    )


def channel_layout(field):
    return lax.all_to_all(field, "ctx", split_axis=0, concat_axis=1, tiled=True)


def by_sequence(field):
    return lax.all_to_all(field, "ctx", split_axis=1, concat_axis=0, tiled=True)


def on_device(tokens, weights, filter_taps, cotangent):
    weight_block = weights
    projected = lax.psum_scatter(
        jnp.einsum("sdc,td->cst", weight_block, tokens, preferred_element_type=jnp.float32).astype(
            jnp.bfloat16
        ),
        "ch",
        scatter_dimension=0,
        tiled=True,
    )
    query = projected[:, 0]
    keys_multiplier = projected[:, 1]
    value_gate = projected[:, 2]
    key_float = keys_multiplier.astype(jnp.float32)
    value_float = value_gate.astype(jnp.float32)
    query_float = query.astype(jnp.float32)
    product = key_float * value_float
    upstream = cotangent.astype(jnp.float32)
    conv_grad = upstream * query_float
    prod_channels = channel_layout(product)
    length = prod_channels.shape[1]
    tap_scale = 1.0 / math.sqrt(length)
    kernel = filter_taps[:, 0, :] * tap_scale
    prod_spec = spectrum(prod_channels)
    kernel_spec = spectrum(kernel)
    conv_channels = inverse(*complex_times(prod_spec, kernel_spec))[:, :length]
    convolved = by_sequence(conv_channels)
    grad_channels = channel_layout(conv_grad)
    grad_spec = spectrum(grad_channels)
    prod_grad_channels = inverse(*complex_conj_times(grad_spec, kernel_spec))[:, :length]
    kernel_grad = inverse(*complex_conj_times(grad_spec, prod_spec))[:, :length] * tap_scale
    prod_grad = by_sequence(prod_grad_channels)
    gated_out = (query_float * convolved).astype(jnp.bfloat16)
    query_grad = upstream * convolved
    grads = jnp.stack([query_grad, prod_grad * value_float, prod_grad * key_float], axis=1).astype(
        jnp.bfloat16
    )
    weight_block = weights
    input_grad = jnp.einsum(
        "cst,sdc->td",
        lax.all_gather(grads, "ch", axis=0, tiled=True),
        weight_block,
        preferred_element_type=jnp.float32,
    ).astype(jnp.bfloat16)
    return (gated_out, input_grad, kernel_grad[:, None, :])


def solution(mesh):
    placed = (P("ctx", "ch"), P(None, "ch", None), P("ctx", "ch", None), P("ch", "ctx"))
    return jax.shard_map(
        on_device,
        mesh=mesh,
        in_specs=placed,
        out_specs=(P("ch", "ctx"), P("ctx", "ch"), P("ctx", "ch", None)),
        check_vma=False,
    )
```

profile of v0, /device:TPU:24, one launch (start us, length us, event | category | flops | bytes accessed | tf_op | source)
XLA Modules:
  0.0 246.2 jit_solution(7441885871840626995)
XLA Ops:
  7.2 1.8 copy-done
  9.1 1.5 fusion
  10.6 1.1 copy.23
  11.7 0.8 multiply_bitcast_fusion
  12.6 0.5 convolution_negate_fusion.1
  13.1 0.5 fusion.86
  13.6 0.7 fusion.84
  14.3 0.7 convolution_add_fusion.4
  15.0 1.3 dynamic-slice
  17.0 0.7 fusion.80
  17.7 0.7 convolution_subtract_fusion.7
  18.4 85.8 %all-reduce.6.cloned.1.call-done = bf16[512,3,128]{2,1,0:T(4,128)(2,1)} async-done(((bf16[512,3,128]{2,1,0:T(4,128)(2,1)}), bf16[512,3,128]{2,1,0:T(4,128)(2,1)}) %all-reduce.6.cloned.1.call-update) | async-done | bytes 393232
  104.2 1.0 constant_dynamic-slice_fusion.1
  105.3 0.6 convert_multiply_fusion.4
  105.9 15.8 %all-to-all-start = ((f32[64,1,128]{2,1,0:T(1,128)}), f32[64,1,128]{2,1,0:T(1,128)S(1)}, u32[]{:S(2)}, u32[]{:S(2)}) async-start(f32[64,1,128]{2,1,0:T(1,128)} %bitcast.3), calls=%async_computation | async-start | bytes 65536 | tf_op jit(solution)/shard_map/all_to_all | solution.py:95
  121.7 0.6 convert_multiply_fusion
  122.3 11.4 %all-to-all-done = f32[64,1,128]{2,1,0:T(1,128)S(1)} async-done(((f32[64,1,128]{2,1,0:T(1,128)}), f32[64,1,128]{2,1,0:T(1,128)S(1)}, u32[]{:S(2)}, u32[]{:S(2)}) %all-to-all-start) | async-done | bytes 32800 | tf_op jit(solution)/shard_map/all_to_all | solution.py:95
  133.7 7.6 %all-to-all-start.2 = ((f32[64,1,128]{2,1,0:T(1,128)}), f32[64,1,128]{2,1,0:T(1,128)S(1)}, u32[]{:S(2)}, u32[]{:S(2)}) async-start(f32[64,1,128]{2,1,0:T(1,128)} %bitcast.15), calls=%async_computation.2 | async-start | bytes 65536 | tf_op jit(solution)/shard_map/all_to_all | solution.py:95
  141.4 0.5 convolution_negate_fusion.2
  141.9 0.5 fusion.90
  142.4 1.3 fusion.88
  143.8 0.7 fusion.82
  144.5 8.8 %all-to-all-done.2 = f32[64,1,128]{2,1,0:T(1,128)S(1)} async-done(((f32[64,1,128]{2,1,0:T(1,128)}), f32[64,1,128]{2,1,0:T(1,128)S(1)}, u32[]{:S(2)}, u32[]{:S(2)}) %all-to-all-start.2) | async-done | bytes 32800 | tf_op jit(solution)/shard_map/all_to_all | solution.py:95
  153.3 0.5 convolution_negate_fusion
  153.9 0.5 fusion.73
  154.4 0.7 fusion.71
  155.1 0.7 fusion.69
  155.8 1.6 convolution_add_fusion.5
  157.4 1.6 convolution_subtract_fusion.8
  159.0 0.7 convolution_add_fusion.2
  159.7 1.2 multiply_add_fusion
  162.5 0.5 convolution_add_fusion
  163.0 0.7 fusion.13
  163.7 0.7 fusion.2
  164.4 0.7 fusion.42
  167.1 0.9 fusion.20
  168.1 0.7 fusion.3
  168.8 0.6 slice_bitcast_fusion
  169.4 7.2 %all-to-all-start.3 = ((f32[1,64,128]{2,0,1:T(1,128)}), f32[1,64,128]{2,0,1:T(1,128)S(1)}, u32[]{:S(2)}, u32[]{:S(2)}) async-start(f32[1,64,128]{2,0,1:T(1,128)} %slice_bitcast_fusion), calls=%async_computation.3 | async-start | bytes 65536 | tf_op jit(solution)/shard_map/all_to_all | solution.py:99
  178.7 0.7 fusion.27
  179.4 0.7 fusion.4
  180.1 0.6 slice_bitcast_fusion.1
  180.7 8.1 %all-to-all-done.3 = f32[1,64,128]{2,0,1:T(1,128)S(1)} async-done(((f32[1,64,128]{2,0,1:T(1,128)}), f32[1,64,128]{2,0,1:T(1,128)S(1)}, u32[]{:S(2)}, u32[]{:S(2)}) %all-to-all-start.3) | async-done | bytes 32800 | tf_op jit(solution)/shard_map/all_to_all | solution.py:99
  188.8 7.3 %all-to-all-start.1 = ((f32[1,64,128]{2,0,1:T(1,128)}), f32[1,64,128]{2,0,1:T(1,128)S(1)}, u32[]{:S(2)}, u32[]{:S(2)}) async-start(f32[1,64,128]{2,0,1:T(1,128)} %slice_bitcast_fusion.1), calls=%async_computation.1 | async-start | bytes 65536 | tf_op jit(solution)/shard_map/all_to_all | solution.py:99
  196.1 12.1 %all-to-all-done.1 = f32[1,64,128]{2,0,1:T(1,128)S(1)} async-done(((f32[1,64,128]{2,0,1:T(1,128)}), f32[1,64,128]{2,0,1:T(1,128)S(1)}, u32[]{:S(2)}, u32[]{:S(2)}) %all-to-all-start.1) | async-done | bytes 32800 | tf_op jit(solution)/shard_map/all_to_all | solution.py:99
  208.2 0.6 fusion.110
  208.8 28.6 %all_gather.3 = bf16[512,3,128]{2,0,1:T(8,128)(2,1)S(1)} all-gather(bf16[64,3,128]{2,0,1:T(8,128)(2,1)S(1)} %pad_maximum_fusion), channel_id=1, replica_groups=mesh['ctx'=64,'ch'=8] {'ch'}, dimensions={0}, use_global_device_ids=true | all-gather | bytes 442368 | tf_op jit(solution)/shard_map/all_gather | solution.py:142
  237.5 1.9 fusion.1
  (27 shorter events, 5.8 us)
Async XLA Ops:
  7.2 1.9 copy-start
  7.2 97.0 %all-reduce.6.cloned.1.call-start = ((), (), s32[]{:S(2)}) async-start(), calls=%async_computation.4 | async-start | bytes 1048576
  10.6 111.1 %copy-start.2 = (bf16[64,128]{1,0:T(8,128)(2,1)S(1)}, bf16[64,128]{1,0:T(8,128)(2,1)}, u32[]{:S(2)}) copy-start(bf16[64,128]{1,0:T(8,128)(2,1)} %param.7) | copy-start | bytes 49156
  105.9 27.9 %all-to-all-start = ((f32[64,1,128]{2,1,0:T(1,128)}), f32[64,1,128]{2,1,0:T(1,128)S(1)}, u32[]{:S(2)}, u32[]{:S(2)}) async-start(f32[64,1,128]{2,1,0:T(1,128)} %bitcast.3), calls=%async_computation | async-start | bytes 65536 | tf_op jit(solution)/shard_map/all_to_all | solution.py:95
  133.7 19.6 %all-to-all-start.2 = ((f32[64,1,128]{2,1,0:T(1,128)}), f32[64,1,128]{2,1,0:T(1,128)S(1)}, u32[]{:S(2)}, u32[]{:S(2)}) async-start(f32[64,1,128]{2,1,0:T(1,128)} %bitcast.15), calls=%async_computation.2 | async-start | bytes 65536 | tf_op jit(solution)/shard_map/all_to_all | solution.py:95
  141.9 1.9 copy-start.4
  142.4 1.4 copy-start.3
  161.0 16.1 %copy-start.1 = (f32[128,128]{1,0:T(8,128)S(1)}, f32[128,128]{1,0:T(8,128)}, u32[]{:S(2)}) copy-start(f32[128,128]{1,0:T(8,128)} %get-tuple-element.18) | copy-start | bytes 196612
  169.4 19.4 %all-to-all-start.3 = ((f32[1,64,128]{2,0,1:T(1,128)}), f32[1,64,128]{2,0,1:T(1,128)S(1)}, u32[]{:S(2)}, u32[]{:S(2)}) async-start(f32[1,64,128]{2,0,1:T(1,128)} %slice_bitcast_fusion), calls=%async_computation.3 | async-start | bytes 65536 | tf_op jit(solution)/shard_map/all_to_all | solution.py:99
  188.8 19.4 %all-to-all-start.1 = ((f32[1,64,128]{2,0,1:T(1,128)}), f32[1,64,128]{2,0,1:T(1,128)S(1)}, u32[]{:S(2)}, u32[]{:S(2)}) async-start(f32[1,64,128]{2,0,1:T(1,128)} %slice_bitcast_fusion.1), calls=%async_computation.1 | async-start | bytes 65536 | tf_op jit(solution)/shard_map/all_to_all | solution.py:99
Sparse Core Ops, SparseCore 0:
  11.8 92.3 all-reduce.5
where the time goes:
time: 250 us; the launch traced here: 246 us
  waiting for transfers between devices  126 us (50%)
  starting transfers between devices  38 us (15%)
  blocking collectives  28.6 us (11%)
  matrix products  28.5 us (11%)
  between operations  15 us (6%)
  local copies, waits for them, and re-layouts  6.58 us (3%)
  other arithmetic  3.31 us (1%)
    unnamed x2, waiting for transfers between devices  85.8 us
    all_gather x1, blocking collectives, on_device(): lax.all_gather(grads, 'ch', axis=0, tiled=True)  28.6 us
    dot_general x36, matrix products, contract(): return jnp.einsum(form, left_side, right_side, precision=highest_precision)  25.1 us
    all_to_all x2, starting transfers between devices, channel_layout(): return lax.all_to_all(field, 'ctx', split_axis=0, concat_axis=1, tiled=True)  23.4 us
    all_to_all x2, waiting for transfers between devices, channel_layout(): return lax.all_to_all(field, 'ctx', split_axis=0, concat_axis=1, tiled=True)  20.2 us
    all_to_all x2, waiting for transfers between devices, by_sequence(): return lax.all_to_all(field, 'ctx', split_axis=1, concat_axis=0, tiled=True)  20.1 us
    all_to_all x2, starting transfers between devices, by_sequence(): return lax.all_to_all(field, 'ctx', split_axis=1, concat_axis=0, tiled=True)  14.6 us
  transfers between devices with their start and end apart: 5, of which 5 were waited for; matrix products, arithmetic and copies ran while one was open for 6% of the time, Pallas kernels for 0%

commit v1 on v0

v1 whole, which is shorter than its diff:
```python
import math

import jax
import jax.numpy as jnp
import numpy as np
from jax import lax
from jax.experimental import pallas as pl
from jax.experimental.pallas import tpu as pltpu
from jax.sharding import Mesh, PartitionSpec as P
import ml_dtypes

F32, BF16 = jnp.float32, jnp.bfloat16
SIDE = 128
LENGTH = 8192
BLOCKS = LENGTH // SIDE
YH, ZC, CH = 2, 32, 8
PLANE = CH * YH
SMALL = pltpu.CompilerParams(vmem_limit_bytes=8 * 1024 * 1024)


def halves(table):
    high = table.astype(ml_dtypes.bfloat16)
    low = (table - high.astype(np.float64)).astype(ml_dtypes.bfloat16)
    return high, low


def make_tables():
    index = np.arange(SIDE)
    angle = 2.0 * np.pi / SIDE * (np.outer(index, index) % SIDE)
    cos, sin = np.cos(angle), np.sin(angle)
    turn = 2.0 * np.pi / (SIDE * SIDE) * np.outer(index, index)
    twiddle = np.stack([np.cos(turn), np.sin(turn)]).astype(np.float32)
    zc, sig, yh = np.meshgrid(np.arange(ZC), np.arange(2), np.arange(YH), indexing="ij")
    block = (yh * ZC + zc).reshape(-1)
    sig = sig.reshape(-1)
    outer = np.concatenate([cos[:, block], -sin[:, block]], axis=0)
    outer = np.concatenate([outer * (sig == 0), outer * (sig == 1)], axis=0)
    outer = np.concatenate(halves(outer), axis=1)
    inner = np.stack(halves(np.block([[cos, -sin], [sin, cos]])))
    real_rows = np.concatenate([cos[block], -sin[block]], axis=1)
    imag_rows = np.concatenate([sin[block], cos[block]], axis=1)
    back = np.stack(halves(np.where((sig == 0)[:, None], real_rows, imag_rows)))
    plain = np.concatenate([cos[:, :BLOCKS], -sin[:, :BLOCKS]], axis=0)
    high, low = halves(plain)
    plain_outer = np.concatenate([high, low, high], axis=1)
    plain_back = np.stack(halves(np.concatenate([cos[:BLOCKS], -sin[:BLOCKS]], axis=1)))
    return outer, twiddle, inner, back, plain_outer, plain_back


def split(value):
    high = value.astype(BF16)
    return high, (value - high.astype(F32)).astype(BF16)


def mul(left, right, rhs_minor=False):
    dims = (((1,), (1 if rhs_minor else 0,)), ((), ()))
    return lax.dot_general(left, right, dims, preferred_element_type=F32)


def times_table(value, table, rhs_minor=False):
    high, low = split(value)
    return (
        mul(high, table[0], rhs_minor) + mul(low, table[0], rhs_minor) + mul(high, table[1], rhs_minor)
    )


def table_times(table, value):
    high, low = split(value)
    return mul(table[0], high) + mul(table[0], low) + mul(table[1], high)


def inner_forward(first, twiddle, inner):
    tc, ts = twiddle[0], twiddle[1]
    rows = []
    for s in range(first.shape[0] // (2 * SIDE)):
        re = first[2 * s * SIDE:(2 * s + 1) * SIDE]
        im = first[(2 * s + 1) * SIDE:(2 * s + 2) * SIDE]
        rows.append(jnp.concatenate([re * tc + im * ts, im * tc - re * ts], axis=1))
    stacked = rows[0] if len(rows) == 1 else jnp.concatenate(rows, axis=0)
    return times_table(stacked, inner)


def inner_backward(spec, twiddle, inner):
    tc, ts = twiddle[0], twiddle[1]
    mid = times_table(spec, inner, rhs_minor=True)
    re, im = mid[:, :SIDE], mid[:, SIDE:]
    return jnp.concatenate([re * tc - im * ts, im * tc + re * ts], axis=0)


def taps_kernel(taps_ref, plain_outer_ref, twiddle_ref, inner_ref, out_ref):
    scale = 1.0 / (math.sqrt(LENGTH) * SIDE * SIDE)
    high, low = split(taps_ref[...] * scale)
    first = mul(plain_outer_ref[...], jnp.concatenate([high, high, low], axis=0))
    out_ref[...] = inner_forward(first, twiddle_ref, inner_ref)


def gate_kernel(parts_ref, fields_ref, send_ref, scratch):
    mine = lax.axis_index("ch")
    for y in range(YH):
        fields = []
        for s in range(3):
            total = parts_ref[y, s].astype(F32)
            for g in range(1, CH):
                total = total + parts_ref[g * YH + y, s].astype(F32)
            rounded = total.astype(BF16)
            fields_ref[y, s] = rounded
            fields.append(rounded.astype(F32))
        upstream = parts_ref[mine * YH + y, 3]
        fields_ref[y, 3] = upstream
        scratch[pl.ds(y, ZC, stride=4), :] = fields[1] * fields[2]
        scratch[pl.ds(2 + y, ZC, stride=4), :] = upstream.astype(F32) * fields[0]
    send_ref[...] = scratch[...].astype(BF16)


def conv_kernel(rows_ref, taps_ref, outer_ref, twiddle_ref, inner_ref, back_ref, spec_ref, send_ref):
    rows = rows_ref[...]
    first = mul(outer_ref[...], jnp.concatenate([rows, rows], axis=0))
    spec = inner_forward(first, twiddle_ref, inner_ref)
    spec_ref[...] = spec
    pr, pi = spec[:SIDE, :SIDE], spec[:SIDE, SIDE:]
    gr, gi = spec[SIDE:, :SIDE], spec[SIDE:, SIDE:]
    kr, ki = taps_ref[:, :SIDE], taps_ref[:, SIDE:]
    re = pr * kr - pi * ki - (gi * kr - gr * ki)
    im = pr * ki + pi * kr + (gr * kr + gi * ki)
    mid = inner_backward(jnp.concatenate([re, im], axis=1), twiddle_ref, inner_ref)
    send_ref[...] = table_times(back_ref, mid).astype(BF16)


def filter_grad_kernel(spec_ref, twiddle_ref, inner_ref, plain_back_ref, out_ref):
    scale = 1.0 / (math.sqrt(LENGTH) * SIDE * SIDE)
    pr, pi = spec_ref[:SIDE, :SIDE], spec_ref[:SIDE, SIDE:]
    gr, gi = spec_ref[SIDE:, :SIDE], spec_ref[SIDE:, SIDE:]
    re = (gr * pr + gi * pi) * scale
    im = (gi * pr - gr * pi) * scale
    mid = inner_backward(jnp.concatenate([re, im], axis=1), twiddle_ref, inner_ref)
    out_ref[...] = table_times(plain_back_ref, mid)


def grads_kernel(rows_ref, fields_ref, send_ref, scratch):
    scratch[...] = rows_ref[...].astype(F32)
    for y in range(YH):
        convolved = scratch[pl.ds(y, ZC, stride=4), :]
        prod_grad = scratch[pl.ds(2 + y, ZC, stride=4), :]
        query, key, value, upstream = (fields_ref[y, s].astype(F32) for s in range(4))
        rows = (upstream * convolved, prod_grad * value, prod_grad * key, query * convolved)
        for s, row in enumerate(rows):
            row = row.astype(BF16)
            for g in range(CH):
                send_ref[g * YH + y, s] = row


def call(kernel, shapes, scratch=()):
    return pl.pallas_call(
        kernel,
        out_shape=shapes,
        compiler_params=SMALL,
        scratch_shapes=list(scratch),
    )


def shape(dims, dtype):
    return jax.ShapeDtypeStruct(dims, dtype)


def exchange(field, axes):
    return lax.all_to_all(field, axes, split_axis=0, concat_axis=0, tiled=True)


def on_device(tokens, weights, filter_taps, cotangent):
    outer, twiddle, inner, back, plain_outer, plain_back = (jnp.asarray(t) for t in make_tables())
    rows = SIDE
    parts = jnp.einsum(
        "sdpc,td->psct", weights.reshape(3, -1, PLANE, 32), tokens, preferred_element_type=F32
    ).astype(BF16)
    upstream = jnp.broadcast_to(
        cotangent.reshape(YH, 1, 32, rows)[None], (CH, YH, 1, 32, rows)
    ).reshape(PLANE, 1, 32, rows)
    parts = exchange(jnp.concatenate([parts, upstream], axis=1), ("ch", "yh"))
    taps = filter_taps.reshape(BLOCKS, SIDE)
    taps_spec = call(taps_kernel, shape((SIDE, 2 * SIDE), F32))(taps, plain_outer, twiddle, inner)
    fields, send = call(
        gate_kernel,
        (shape((YH, 4, 32, rows), BF16), shape((SIDE, SIDE), BF16)),
        [pltpu.VMEM((SIDE, SIDE), F32)],
    )(parts)
    arrived = exchange(send.reshape(ZC, 4, SIDE), "zc").reshape(SIDE, SIDE)
    spec, send = call(
        conv_kernel, (shape((2 * SIDE, 2 * SIDE), F32), shape((SIDE, SIDE), BF16))
    )(arrived, taps_spec, outer, twiddle, inner, back)
    arrived = exchange(send.reshape(ZC, 4, SIDE), "zc").reshape(SIDE, SIDE)
    kernel_grad = call(filter_grad_kernel, shape((BLOCKS, SIDE), F32))(
        spec, twiddle, inner, plain_back
    )
    grads = call(
        grads_kernel, shape((PLANE, 4, 32, rows), BF16), [pltpu.VMEM((SIDE, SIDE), F32)]
    )(arrived, fields)
    grads = exchange(grads, ("ch", "yh"))
    input_grad = jnp.einsum(
        "psct,sdpc->td",
        grads[:, :3],
        weights.reshape(3, -1, PLANE, 32),
        preferred_element_type=F32,
    ).astype(BF16)
    mine = lax.axis_index("ch")
    gated_out = lax.dynamic_slice_in_dim(grads[:, 3], mine * YH, YH, axis=0).reshape(2 * 32, rows)
    return gated_out, input_grad, kernel_grad.reshape(1, 1, LENGTH)


def solution(mesh):
    view = Mesh(mesh.devices.reshape(YH, ZC, CH), ("yh", "zc", "ch"))
    ctx = ("yh", "zc")
    return jax.shard_map(
        on_device,
        mesh=view,
        in_specs=(P(ctx, "ch"), P(None, "ch", None), P(ctx, "ch", None), P("ch", ctx)),
        out_specs=(P("ch", ctx), P(ctx, "ch"), P(ctx, "ch", None)),
        check_vma=False,
    )
```

time: 250 us -> 92.3 us (0.37)
  waiting for transfers between devices: 126 us -> 20.6 us
  matrix products: 28.5 us -> 6.13 us
  starting transfers between devices: 38 us -> 21.2 us
  between operations: 15 us -> 0.79 us
  Pallas kernels: 0 us -> 4.05 us
  blocking collectives: 28.6 us -> 32.5 us
  other arithmetic: 3.31 us -> 0.05 us
    unnamed x2 -> x0, waiting for transfers between devices: 85.8 us -> none
    all_to_all x0 -> x2, blocking collectives: none -> 32.5 us  [exchange(): return lax.all_to_all(field, axes, split_axis=0, concat_axis=0, tiled=True)]
    all_gather x1 -> x0, blocking collectives: 28.6 us -> none  [on_device(): lax.all_gather(grads, 'ch', axis=0, tiled=True)]
    dot_general x38 -> x1, matrix products: 28.5 us -> 3.2 us  [on_device(): jnp.einsum('psct,sdpc->td', grads[:, :3], weights.reshape(3, -1, PLANE, 3...]
    all_to_all x4 -> x2, waiting for transfers between devices: 40.3 us -> 20.6 us  [exchange(): return lax.all_to_all(field, axes, split_axis=0, concat_axis=0, tiled=True)]
    all_to_all x4 -> x2, starting transfers between devices: 38 us -> 21.2 us  [exchange(): return lax.all_to_all(field, axes, split_axis=0, concat_axis=0, tiled=True)]
    pallas_call x0 -> x5, Pallas kernels: none -> 4.05 us  [the longest x1 1.09 us: on_device(): call(filter_grad_kernel, shape((BLOCKS, SIDE), F32))]
    unnamed x0 -> x1, matrix products: none -> 2.92 us
  transfers between devices with their start and end apart: 5 -> 2, of which waited for: 5 -> 2; matrix products, arithmetic and copies ran while one was open for 6% -> 0% of each run, Pallas kernels for 0% -> 2%
where the time goes in v1:
time: 92.3 us; the launch traced here: 90.7 us
  blocking collectives  32.5 us (35%)
  starting transfers between devices  21.2 us (23%)
  waiting for transfers between devices  20.6 us (22%)
  matrix products  6.13 us (7%)
  local copies, waits for them, and re-layouts  5.5 us (6%)
  Pallas kernels  4.05 us (4%)
    all_to_all x2, blocking collectives, exchange(): return lax.all_to_all(field, axes, split_axis=0, concat_axis=0, tiled=True)  32.5 us
    all_to_all x2, starting transfers between devices, exchange(): return lax.all_to_all(field, axes, split_axis=0, concat_axis=0, tiled=True)  21.2 us
    all_to_all x2, waiting for transfers between devices, exchange(): return lax.all_to_all(field, axes, split_axis=0, concat_axis=0, tiled=True)  20.6 us
    unnamed x19, local copies, waits for them, and re-layouts  4.79 us
    dot_general x1, matrix products, on_device(): jnp.einsum('psct,sdpc->td', grads[:, :3], weights.reshape(3, -1, PLANE, 3...  3.2 us
    unnamed x1, matrix products  2.92 us
  transfers between devices with their start and end apart: 2, of which 2 were waited for; matrix products, arithmetic and copies ran while one was open for 0% of the time, Pallas kernels for 2%

profile of v1, /device:TPU:24, one launch (start us, length us, event | category | flops | bytes accessed | tf_op | source)
XLA Modules:
  0.0 90.7 jit_solution(11345080306864229242)
XLA Ops:
  0.6 0.0 copy-start
  0.6 4.7 %copy.16 = bf16[3,1024,512]{1,2,0:T(8,128)(2,1)} copy(bf16[3,1024,512]{2,1,0:T(8,128)(2,1)} %param.11) | data formatting | bytes 6291456 | tf_op args[1]
  5.4 0.0 copy-start.8
  5.4 0.0 copy-done
  5.4 0.0 copy-start.1
  5.4 0.0 copy-start.2
  5.4 0.0 copy-start.4
  5.4 0.0 copy-start.7
  5.4 2.9 %fusion.9 = f32[128,1536]{0,1:S(1)} fusion(bf16[128,1024]{1,0:T(8,128)(2,1)S(1)} %copy-done, bf16[1024,1536]{0,1:T(8,128)(2,1)} %bitcast.31), kind=kOutput, calls=%fused_computation.8 | convolution fusion | flops 402653184 | bytes 4194304
  8.4 0.0 copy-start.3
  8.4 0.0 copy-start.5
  8.4 0.1 copy.29
  8.4 0.0 copy-start.6
  8.5 0.0 copy-done.8
  8.5 0.1 pad_maximum_fusion
  8.6 16.6 %all_to_all.20.parts_ref = bf16[16,4,32,128]{3,2,1,0:T(8,128)(2,1)S(1)} all-to-all(bf16[16,4,32,128]{3,2,1,0:T(8,128)(2,1)S(1)} %pad_maximum_fusion), channel_id=1, replica_groups=mesh['yh'=2,'zc'=32,'ch'=8] {'ch','yh'}, dimensions={0} | all-to-all | bytes 1048576 | tf_op jit(solution)/shard_map/all_to_all | solution.py:166
  25.1 0.7 shard_map.121
  25.8 15.5 %all-to-all-start.1 = ((bf16[32,4,128]{2,1,0:T(4,128)(2,1)}), bf16[32,4,128]{2,1,0:T(4,128)(2,1)S(1)}, u32[]{:S(2)}, u32[]{:S(2)}) async-start(bf16[32,4,128]{2,1,0:T(4,128)(2,1)} %bitcast.7), calls=%async_computation.1 | async-start | bytes 65536 | tf_op jit(solution)/shard_map/all_to_all | solution.py:166
  41.3 0.0 copy-done.1
  41.4 0.0 copy-done.2
  41.4 0.0 copy-done.4
  41.4 0.0 copy-done.7
  41.4 0.4 shard_map.122.taps_ref
  41.8 12.6 %all-to-all-done.1 = bf16[32,4,128]{2,1,0:T(4,128)(2,1)S(1)} async-done(((bf16[32,4,128]{2,1,0:T(4,128)(2,1)}), bf16[32,4,128]{2,1,0:T(4,128)(2,1)S(1)}, u32[]{:S(2)}, u32[]{:S(2)}) %all-to-all-start.1) | async-done | bytes 32800 | tf_op jit(solution)/shard_map/all_to_all | solution.py:166
  54.3 0.0 copy-done.3
  54.3 0.0 copy-done.5
  54.4 1.0 %shard_map.123 = (f32[256,256]{1,0:T(8,128)S(1)}, bf16[128,128]{1,0:T(8,128)(2,1)S(1)}) custom-call(bf16[128,128]{1,0:T(8,128)(2,1)S(1)} %bitcast.28, f32[128,256]{1,0:T(8,128)S(1)} %shard_map.122.taps_ref, bf16[512,256]{1,0:T(8,128)(2,1)S(1)} %copy-done.3, f32[2,128,128]{2,1,0:T(8,128)S(1)} %copy-done.2, bf16[2,256,256]{2,1,0:T(8,128)(2,1)S(1)} %copy-done.1, ...), custom_call_target="tpu_custom_call" | custom-call | tf_op jit(solution)/shard_map/pallas_call | solution.py:187
  55.4 15.9 %all_to_all.21 = bf16[32,4,128]{2,1,0:T(4,128)(2,1)S(1)} all-to-all(bf16[32,4,128]{2,1,0:T(4,128)(2,1)S(1)} %bitcast.29), channel_id=1, replica_groups=mesh['yh'=2,'zc'=32,'ch'=8] {'zc'}, dimensions={0} | all-to-all | bytes 65536 | tf_op jit(solution)/shard_map/all_to_all | solution.py:166
  71.3 0.9 shard_map.124
  72.2 5.6 %all-to-all-start.3 = ((bf16[16,4,32,128]{3,2,1,0:T(8,128)(2,1)}), bf16[16,4,32,128]{3,2,1,0:T(8,128)(2,1)S(1)}, u32[]{:S(2)}, u32[]{:S(2)}) async-start(bf16[16,4,32,128]{3,2,1,0:T(8,128)(2,1)} %shard_map.124), calls=%async_computation.3 | async-start | bytes 1048576 | tf_op jit(solution)/shard_map/all_to_all | solution.py:166
  77.8 0.0 copy-done.6
  77.8 1.1 %shard_map.125 = f32[64,128]{1,0:T(8,128)} custom-call(f32[256,256]{1,0:T(8,128)S(1)} %get-tuple-element.10.spec_ref, f32[2,128,128]{2,1,0:T(8,128)S(1)} %copy-done.2, bf16[2,256,256]{2,1,0:T(8,128)(2,1)S(1)} %copy-done.1, bf16[2,64,256]{2,1,0:T(8,128)(2,1)S(1)} %copy-done.6), custom_call_target="tpu_custom_call" | custom-call | tf_op jit(solution)/shard_map/pallas_call | solution.py:191
  78.9 8.0 %all-to-all-done.3 = bf16[16,4,32,128]{3,2,1,0:T(8,128)(2,1)S(1)} async-done(((bf16[16,4,32,128]{3,2,1,0:T(8,128)(2,1)}), bf16[16,4,32,128]{3,2,1,0:T(8,128)(2,1)S(1)}, u32[]{:S(2)}, u32[]{:S(2)}) %all-to-all-start.3) | async-done | bytes 524320 | tf_op jit(solution)/shard_map/all_to_all | solution.py:166
  86.9 0.6 constant_dynamic-slice_fusion
  87.5 3.2 %fusion.5 = bf16[128,1024]{1,0:T(8,128)(2,1)} fusion(bf16[16,4,32,128]{3,2,1,0:T(8,128)(2,1)S(1)} %all-to-all-done.3, bf16[3,1024,16,32]{1,3,2,0:T(8,128)(2,1)} %bitcast.32), kind=kOutput, calls=%fused_computation.3 | convolution fusion | flops 402784256 | bytes 3932160 | tf_op jit(solution)/shard_map/psct,sdpc->td/dot_general | solution.py:198
  (2 shorter events, 0.0 us)
Async XLA Ops:
  0.6 4.8 %copy-start = (bf16[128,1024]{1,0:T(8,128)(2,1)S(1)}, bf16[128,1024]{1,0:T(8,128)(2,1)}, u32[]{:S(2)}) copy-start(bf16[128,1024]{1,0:T(8,128)(2,1)} %param.10) | copy-start | bytes 786436
  5.4 3.1 %copy-start.8 = (bf16[64,128]{1,0:T(8,128)(2,1)S(1)}, bf16[64,128]{1,0:T(8,128)(2,1)}, u32[]{:S(2)}) copy-start(bf16[64,128]{1,0:T(8,128)(2,1)} %param.13) | copy-start | bytes 49156
  5.4 36.0 %copy-start.1 = (bf16[2,256,256]{2,1,0:T(8,128)(2,1)S(1)}, bf16[2,256,256]{2,1,0:T(8,128)(2,1)}, u32[]{:S(2)}) copy-start(bf16[2,256,256]{2,1,0:T(8,128)(2,1)} %constant.25.clone.inner_ref) | copy-start | bytes 786436
  5.4 36.0 %copy-start.2 = (f32[2,128,128]{2,1,0:T(8,128)S(1)}, f32[2,128,128]{2,1,0:T(8,128)}, u32[]{:S(2)}) copy-start(f32[2,128,128]{2,1,0:T(8,128)} %constant.24.clone.twiddle_ref) | copy-start | bytes 393220
  5.4 36.0 %copy-start.4 = (bf16[256,192]{1,0:T(8,128)(2,1)S(1)}, bf16[256,192]{1,0:T(8,128)(2,1)}, u32[]{:S(2)}) copy-start(bf16[256,192]{1,0:T(8,128)(2,1)} %constant.27.clone.plain_outer_ref) | copy-start | bytes 294916
  5.4 36.0 %copy-start.7 = (f32[1,1,8192]{2,1,0:T(1,128)S(1)}, f32[1,1,8192]{2,1,0:T(1,128)}, u32[]{:S(2)}) copy-start(f32[1,1,8192]{2,1,0:T(1,128)} %param.12) | copy-start | bytes 98308
  8.4 46.0 %copy-start.3 = (bf16[512,256]{1,0:T(8,128)(2,1)S(1)}, bf16[512,256]{1,0:T(8,128)(2,1)}, u32[]{:S(2)}) copy-start(bf16[512,256]{1,0:T(8,128)(2,1)} %constant.23.clone.outer_ref) | copy-start | bytes 786436
  8.4 46.0 %copy-start.5 = (bf16[2,128,256]{2,1,0:T(8,128)(2,1)S(1)}, bf16[2,128,256]{2,1,0:T(8,128)(2,1)}, u32[]{:S(2)}) copy-start(bf16[2,128,256]{2,1,0:T(8,128)(2,1)} %constant.26.clone.back_ref) | copy-start | bytes 393220
  8.4 69.4 %copy-start.6 = (bf16[2,64,256]{2,1,0:T(8,128)(2,1)S(1)}, bf16[2,64,256]{2,1,0:T(8,128)(2,1)}, u32[]{:S(2)}) copy-start(bf16[2,64,256]{2,1,0:T(8,128)(2,1)} %constant.28.clone.plain_back_ref) | copy-start | bytes 196612
  25.8 28.5 %all-to-all-start.1 = ((bf16[32,4,128]{2,1,0:T(4,128)(2,1)}), bf16[32,4,128]{2,1,0:T(4,128)(2,1)S(1)}, u32[]{:S(2)}, u32[]{:S(2)}) async-start(bf16[32,4,128]{2,1,0:T(4,128)(2,1)} %bitcast.7), calls=%async_computation.1 | async-start | bytes 65536 | tf_op jit(solution)/shard_map/all_to_all | solution.py:166
  72.2 14.7 %all-to-all-start.3 = ((bf16[16,4,32,128]{3,2,1,0:T(8,128)(2,1)}), bf16[16,4,32,128]{3,2,1,0:T(8,128)(2,1)S(1)}, u32[]{:S(2)}, u32[]{:S(2)}) async-start(bf16[16,4,32,128]{3,2,1,0:T(8,128)(2,1)} %shard_map.124), calls=%async_computation.3 | async-start | bytes 1048576 | tf_op jit(solution)/shard_map/all_to_all | solution.py:166

commit v2 on v1

--- a/solution.py
+++ b/solution.py
@@ -15,6 +15,7 @@
 BLOCKS = LENGTH // SIDE
 YH, ZC, CH = 2, 32, 8
 PLANE = CH * YH
+LARGE = pltpu.CompilerParams(vmem_limit_bytes=20 * 1024 * 1024)
 SMALL = pltpu.CompilerParams(vmem_limit_bytes=8 * 1024 * 1024)
 
 
@@ -87,11 +88,37 @@
     return jnp.concatenate([re * tc - im * ts, im * tc + re * ts], axis=0)
 
 
-def taps_kernel(taps_ref, plain_outer_ref, twiddle_ref, inner_ref, out_ref):
+def taps_spectrum(taps, plain_outer, twiddle, inner):
     scale = 1.0 / (math.sqrt(LENGTH) * SIDE * SIDE)
-    high, low = split(taps_ref[...] * scale)
-    first = mul(plain_outer_ref[...], jnp.concatenate([high, high, low], axis=0))
-    out_ref[...] = inner_forward(first, twiddle_ref, inner_ref)
+    high, low = split(taps * scale)
+    first = mul(plain_outer, jnp.concatenate([high, high, low], axis=0))
+    return inner_forward(first, twiddle, inner)
+
+
+def project_kernel(*refs):
+    sources, (send_ref, spec_ref), held, sems = refs[:7], refs[7:9], refs[9:16], refs[16]
+    plain_outer, twiddle, inner, taps, cotangent, tokens, weights = held
+    copies = [
+        pltpu.make_async_copy(source, target, sems.at[i])
+        for i, (source, target) in enumerate(zip(sources[:6], held[:6]))
+    ] + [
+        pltpu.make_async_copy(sources[6].at[s], weights.at[s], sems.at[6 + s]) for s in range(3)
+    ]
+    for copy in copies:
+        copy.start()
+    for copy in copies[:5]:
+        copy.wait()
+    for y in range(YH):
+        upstream = cotangent[32 * y:32 * y + 32]
+        for g in range(CH):
+            send_ref[g * YH + y, 3] = upstream
+    spec_ref[...] = taps_spectrum(taps[...], plain_outer[...], twiddle, inner)
+    copies[5].wait()
+    for s in range(3):
+        copies[6 + s].wait()
+        part = mul(tokens[...], weights[s]).T.astype(BF16)
+        for p in range(PLANE):
+            send_ref[p, s] = part[32 * p:32 * p + 32]
 
 
 def gate_kernel(parts_ref, fields_ref, send_ref, scratch):
@@ -126,14 +153,30 @@
     send_ref[...] = table_times(back_ref, mid).astype(BF16)
 
 
-def filter_grad_kernel(spec_ref, twiddle_ref, inner_ref, plain_back_ref, out_ref):
+def filter_grad(spec_ref, twiddle_ref, inner_ref, plain_back_ref):
     scale = 1.0 / (math.sqrt(LENGTH) * SIDE * SIDE)
     pr, pi = spec_ref[:SIDE, :SIDE], spec_ref[:SIDE, SIDE:]
     gr, gi = spec_ref[SIDE:, :SIDE], spec_ref[SIDE:, SIDE:]
     re = (gr * pr + gi * pi) * scale
     im = (gi * pr - gr * pi) * scale
     mid = inner_backward(jnp.concatenate([re, im], axis=1), twiddle_ref, inner_ref)
-    out_ref[...] = table_times(plain_back_ref, mid)
+    return table_times(plain_back_ref, mid)
+
+
+def finish_kernel(
+    grads_ref, weights_ref, spec_ref, twiddle_ref, inner_ref, plain_back_ref,
+    gated_ref, input_ref, filter_ref,
+):
+    filter_ref[...] = filter_grad(spec_ref, twiddle_ref, inner_ref, plain_back_ref)
+    mine = lax.axis_index("ch")
+    for y in range(YH):
+        gated_ref[32 * y:32 * y + 32] = grads_ref[mine * YH + y, 3]
+    total = None
+    for s in range(3):
+        rows = jnp.concatenate([grads_ref[p, s] for p in range(PLANE)], axis=0)
+        part = mul(rows.T, weights_ref[s], rhs_minor=True)
+        total = part if total is None else total + part
+    input_ref[...] = total.astype(BF16)
 
 
 def grads_kernel(rows_ref, fields_ref, send_ref, scratch):
@@ -149,12 +192,9 @@
                 send_ref[g * YH + y, s] = row
 
 
-def call(kernel, shapes, scratch=()):
+def call(kernel, shapes, scratch=(), params=SMALL, **extra):
     return pl.pallas_call(
-        kernel,
-        out_shape=shapes,
-        compiler_params=SMALL,
-        scratch_shapes=list(scratch),
+        kernel, out_shape=shapes, compiler_params=params, scratch_shapes=list(scratch), **extra
     )
 
 
@@ -169,15 +209,17 @@
 def on_device(tokens, weights, filter_taps, cotangent):
     outer, twiddle, inner, back, plain_outer, plain_back = (jnp.asarray(t) for t in make_tables())
     rows = SIDE
-    parts = jnp.einsum(
-        "sdpc,td->psct", weights.reshape(3, -1, PLANE, 32), tokens, preferred_element_type=F32
-    ).astype(BF16)
-    upstream = jnp.broadcast_to(
-        cotangent.reshape(YH, 1, 32, rows)[None], (CH, YH, 1, 32, rows)
-    ).reshape(PLANE, 1, 32, rows)
-    parts = exchange(jnp.concatenate([parts, upstream], axis=1), ("ch", "yh"))
-    taps = filter_taps.reshape(BLOCKS, SIDE)
-    taps_spec = call(taps_kernel, shape((SIDE, 2 * SIDE), F32))(taps, plain_outer, twiddle, inner)
+    operands = (
+        plain_outer, twiddle, inner, filter_taps.reshape(BLOCKS, SIDE), cotangent, tokens, weights
+    )
+    parts, taps_spec = call(
+        project_kernel,
+        (pltpu.VMEM((PLANE, 4, 32, rows), BF16), pltpu.VMEM((SIDE, 2 * SIDE), F32)),
+        [pltpu.VMEM(t.shape, t.dtype) for t in operands] + [pltpu.SemaphoreType.DMA((9,))],
+        LARGE,
+        in_specs=[pl.BlockSpec(memory_space=pltpu.HBM)] * 7,
+    )(*(pltpu.with_memory_space_constraint(t, pltpu.HBM) for t in operands))
+    parts = exchange(parts, ("ch", "yh"))
     fields, send = call(
         gate_kernel,
         (shape((YH, 4, 32, rows), BF16), shape((SIDE, SIDE), BF16)),
@@ -188,21 +230,14 @@
         conv_kernel, (shape((2 * SIDE, 2 * SIDE), F32), shape((SIDE, SIDE), BF16))
     )(arrived, taps_spec, outer, twiddle, inner, back)
     arrived = exchange(send.reshape(ZC, 4, SIDE), "zc").reshape(SIDE, SIDE)
-    kernel_grad = call(filter_grad_kernel, shape((BLOCKS, SIDE), F32))(
-        spec, twiddle, inner, plain_back
-    )
     grads = call(
         grads_kernel, shape((PLANE, 4, 32, rows), BF16), [pltpu.VMEM((SIDE, SIDE), F32)]
     )(arrived, fields)
     grads = exchange(grads, ("ch", "yh"))
-    input_grad = jnp.einsum(
-        "psct,sdpc->td",
-        grads[:, :3],
-        weights.reshape(3, -1, PLANE, 32),
-        preferred_element_type=F32,
-    ).astype(BF16)
-    mine = lax.axis_index("ch")
-    gated_out = lax.dynamic_slice_in_dim(grads[:, 3], mine * YH, YH, axis=0).reshape(2 * 32, rows)
+    gated_out, input_grad, kernel_grad = call(
+        finish_kernel,
+        (shape((2 * 32, rows), BF16), shape(tokens.shape, BF16), shape((BLOCKS, SIDE), F32)),
+    )(grads, weights, spec, twiddle, inner, plain_back)
     return gated_out, input_grad, kernel_grad.reshape(1, 1, LENGTH)
 
 

time: 92.3 us -> 83.9 us (0.909)
  blocking collectives: 32.5 us -> 75.6 us
  starting transfers between devices: 21.2 us -> 0 us
  waiting for transfers between devices: 20.6 us -> 0 us
  matrix products: 6.13 us -> 0 us
  local copies, waits for them, and re-layouts: 5.5 us -> 0.04 us
  Pallas kernels: 4.05 us -> 6.22 us
    all_to_all x2 -> x4, blocking collectives: 32.5 us -> 75.6 us  [exchange(): return lax.all_to_all(field, axes, split_axis=0, concat_axis=0, tiled=True)]
    all_to_all x2 -> x0, starting transfers between devices: 21.2 us -> none  [exchange(): return lax.all_to_all(field, axes, split_axis=0, concat_axis=0, tiled=True)]
    all_to_all x2 -> x0, waiting for transfers between devices: 20.6 us -> none  [exchange(): return lax.all_to_all(field, axes, split_axis=0, concat_axis=0, tiled=True)]
    unnamed x19 -> x12, local copies, waits for them, and re-layouts: 4.79 us -> 0.04 us
    pallas_call x2, Pallas kernels: 1.48 us -> 5.08 us  [the longest x1 2.87 us: on_device(): call(project_kernel, (pltpu.VMEM((PLANE, 4, 32, rows), BF16), pltpu.VMEM(...]
    dot_general x1 -> x0, matrix products: 3.2 us -> none  [on_device(): jnp.einsum('psct,sdpc->td', grads[:, :3], weights.reshape(3, -1, PLANE, 3...]
    unnamed x1 -> x0, matrix products: 2.92 us -> none
  transfers between devices with their start and end apart: 2 -> 0, of which waited for: 2 -> 0; matrix products, arithmetic and copies ran while one was open for 0% -> 0% of each run, Pallas kernels for 2% -> 0%
where the time goes in v2:
time: 83.9 us; the launch traced here: 82.6 us
  blocking collectives  75.6 us (90%)
  Pallas kernels  6.22 us (7%)
    all_to_all x4, blocking collectives, exchange(): return lax.all_to_all(field, axes, split_axis=0, concat_axis=0, tiled=True)  75.6 us
    pallas_call x1, Pallas kernels, on_device(): call(project_kernel, (pltpu.VMEM((PLANE, 4, 32, rows), BF16), pltpu.VMEM(...  2.87 us
    pallas_call x1, Pallas kernels, on_device(): call(finish_kernel, (shape((2 * 32, rows), BF16), shape(tokens.shape, BF1...  2.21 us

profile of v2, /device:TPU:24, one launch (start us, length us, event | category | flops | bytes accessed | tf_op | source)
XLA Modules:
  0.0 82.6 jit_solution(17612393210990170751)
XLA Ops:
  0.6 0.0 copy-start.1
  0.6 0.0 copy-start.2
  0.7 0.0 copy-start.4
  0.7 0.0 copy-start.3
  0.7 2.9 %shard_map.121 = (bf16[16,4,32,128]{3,2,1,0:T(8,128)(2,1)S(1)}, f32[128,256]{1,0:T(8,128)S(1)}) custom-call(bf16[256,192]{1,0:T(8,128)(2,1)} %constant.16.clone.refs_0_, f32[2,128,128]{2,1,0:T(8,128)} %constant.13.clone.refs_1_.twiddle_ref, bf16[2,256,256]{2,1,0:T(8,128)(2,1)} %constant.14.clone.refs_2_.inner_ref, f32[64,128]{1,0:T(8,128)} %bitcast.10, ...), custom_call_target="tpu_custom_call" | custom-call | tf_op jit(solution)/shard_map/pallas_call | solution.py:215
  3.6 0.0 copy-start
  3.6 0.0 copy-start.5
  3.6 16.8 %all_to_all.20.parts_ref = bf16[16,4,32,128]{3,2,1,0:T(8,128)(2,1)S(1)} all-to-all(bf16[16,4,32,128]{3,2,1,0:T(8,128)(2,1)S(1)} %get-tuple-element.12), channel_id=1, replica_groups=mesh['yh'=2,'zc'=32,'ch'=8] {'ch','yh'}, dimensions={0} | all-to-all | bytes 1048576 | tf_op jit(solution)/shard_map/all_to_all | solution.py:206
  20.4 0.1 shard_map.122
  20.5 28.3 %all_to_all.21 = bf16[32,4,128]{2,1,0:T(4,128)(2,1)S(1)} all-to-all(bf16[32,4,128]{2,1,0:T(4,128)(2,1)S(1)} %bitcast.9), channel_id=1, replica_groups=mesh['yh'=2,'zc'=32,'ch'=8] {'zc'}, dimensions={0} | all-to-all | bytes 65536 | tf_op jit(solution)/shard_map/all_to_all | solution.py:206
  48.8 0.0 copy-done.1
  48.8 0.0 copy-done.2
  48.8 0.0 copy-done.4
  48.8 0.0 copy-done.3
  48.8 1.0 %shard_map.123 = (f32[256,256]{1,0:T(8,128)S(1)}, bf16[128,128]{1,0:T(8,128)(2,1)S(1)}) custom-call(bf16[128,128]{1,0:T(8,128)(2,1)S(1)} %bitcast.7, f32[128,256]{1,0:T(8,128)S(1)} %get-tuple-element.14.taps_ref, bf16[512,256]{1,0:T(8,128)(2,1)S(1)} %copy-done.3, f32[2,128,128]{2,1,0:T(8,128)S(1)} %copy-done.2, bf16[2,256,256]{2,1,0:T(8,128)(2,1)S(1)} %copy-done.1, ...), custom_call_target="tpu_custom_call" | custom-call | tf_op jit(solution)/shard_map/pallas_call | solution.py:229
  49.9 15.9 %all_to_all.22 = bf16[32,4,128]{2,1,0:T(4,128)(2,1)S(1)} all-to-all(bf16[32,4,128]{2,1,0:T(4,128)(2,1)S(1)} %bitcast.8), channel_id=1, replica_groups=mesh['yh'=2,'zc'=32,'ch'=8] {'zc'}, dimensions={0} | all-to-all | bytes 65536 | tf_op jit(solution)/shard_map/all_to_all | solution.py:206
  65.9 14.5 %all_to_all.23.grads_ref = bf16[16,4,32,128]{3,2,1,0:T(8,128)(2,1)S(1)} all-to-all(bf16[16,4,32,128]{3,2,1,0:T(8,128)(2,1)S(1)} %shard_map.124), channel_id=1, replica_groups=mesh['yh'=2,'zc'=32,'ch'=8] {'ch','yh'}, dimensions={0} | all-to-all | bytes 1048576 | tf_op jit(solution)/shard_map/all_to_all | solution.py:206
  80.4 0.0 copy-done
  80.4 0.0 copy-done.5
  80.4 2.2 %shard_map.125 = (bf16[64,128]{1,0:T(8,128)(2,1)}, bf16[128,1024]{1,0:T(8,128)(2,1)}, f32[64,128]{1,0:T(8,128)}) custom-call(bf16[16,4,32,128]{3,2,1,0:T(8,128)(2,1)S(1)} %all_to_all.23.grads_ref, bf16[3,1024,512]{2,1,0:T(8,128)(2,1)S(1)} %copy-done, f32[256,256]{1,0:T(8,128)S(1)} %get-tuple-element.17.spec_ref, f32[2,128,128]{2,1,0:T(8,128)S(1)} %copy-done.2, ...), custom_call_target="tpu_custom_call" | custom-call | tf_op jit(solution)/shard_map/pallas_call | solution.py:237
  (1 shorter events, 0.0 us)
Async XLA Ops:
  0.6 48.2 %copy-start.1 = (bf16[2,256,256]{2,1,0:T(8,128)(2,1)S(1)}, bf16[2,256,256]{2,1,0:T(8,128)(2,1)}, u32[]{:S(2)}) copy-start(bf16[2,256,256]{2,1,0:T(8,128)(2,1)} %constant.14.clone.refs_2_.inner_ref) | copy-start | bytes 786436
  0.6 48.2 %copy-start.2 = (f32[2,128,128]{2,1,0:T(8,128)S(1)}, f32[2,128,128]{2,1,0:T(8,128)}, u32[]{:S(2)}) copy-start(f32[2,128,128]{2,1,0:T(8,128)} %constant.13.clone.refs_1_.twiddle_ref) | copy-start | bytes 393220
  0.7 48.2 %copy-start.4 = (bf16[2,128,256]{2,1,0:T(8,128)(2,1)S(1)}, bf16[2,128,256]{2,1,0:T(8,128)(2,1)}, u32[]{:S(2)}) copy-start(bf16[2,128,256]{2,1,0:T(8,128)(2,1)} %constant.15.clone.back_ref) | copy-start | bytes 393220
  0.7 48.2 %copy-start.3 = (bf16[512,256]{1,0:T(8,128)(2,1)S(1)}, bf16[512,256]{1,0:T(8,128)(2,1)}, u32[]{:S(2)}) copy-start(bf16[512,256]{1,0:T(8,128)(2,1)} %constant.12.clone.outer_ref) | copy-start | bytes 786436
  3.6 76.8 %copy-start = (bf16[3,1024,512]{2,1,0:T(8,128)(2,1)S(1)}, bf16[3,1024,512]{2,1,0:T(8,128)(2,1)}, u32[]{:S(2)}) copy-start(bf16[3,1024,512]{2,1,0:T(8,128)(2,1)} %weights_ref.1) | copy-start | bytes 9437188
  3.6 76.8 %copy-start.5 = (bf16[2,64,256]{2,1,0:T(8,128)(2,1)S(1)}, bf16[2,64,256]{2,1,0:T(8,128)(2,1)}, u32[]{:S(2)}) copy-start(bf16[2,64,256]{2,1,0:T(8,128)(2,1)} %constant.17.clone.plain_back_ref) | copy-start | bytes 196612

commit v3 on v2

v3 whole, which is shorter than its diff:
```python
import math

import jax
import jax.numpy as jnp
import numpy as np
from jax import lax
from jax.experimental import pallas as pl
from jax.experimental.pallas import tpu as pltpu
from jax.sharding import PartitionSpec as P
import ml_dtypes

F32, BF16 = jnp.float32, jnp.bfloat16
SIDE = 128
LENGTH = 8192
BLOCKS = LENGTH // SIDE
CTX, CH = 64, 8
GROUP = 64


def led_by(first, size):
    order = list(range(size))
    order[0], order[first] = first, 0
    return order


CTX_FIRST, CH_FIRST = 54, 7
CTX_ORDER, CH_ORDER = led_by(CTX_FIRST, CTX), led_by(CH_FIRST, CH)
LARGE = pltpu.CompilerParams(vmem_limit_bytes=20 * 1024 * 1024)
SMALL = pltpu.CompilerParams(vmem_limit_bytes=8 * 1024 * 1024)


def halves(table):
    high = table.astype(ml_dtypes.bfloat16)
    low = (table - high.astype(np.float64)).astype(ml_dtypes.bfloat16)
    return high, low


def make_tables():
    index = np.arange(SIDE)
    angle = 2.0 * np.pi / SIDE * (np.outer(index, index) % SIDE)
    cos, sin = np.cos(angle), np.sin(angle)
    turn = 2.0 * np.pi / (SIDE * SIDE) * np.outer(index, index)
    twiddle = np.stack([np.cos(turn), np.sin(turn)]).astype(np.float32)
    block = np.repeat(np.array(CTX_ORDER), 2)
    sig = np.tile(np.arange(2), CTX)
    outer = np.concatenate([cos[:, block], -sin[:, block]], axis=0)
    outer = np.concatenate([outer * (sig == 0), outer * (sig == 1)], axis=0)
    outer = np.concatenate(halves(outer), axis=1)
    inner = np.stack(halves(np.block([[cos, -sin], [sin, cos]])))
    real_rows = np.concatenate([cos[block], -sin[block]], axis=1)
    imag_rows = np.concatenate([sin[block], cos[block]], axis=1)
    back = np.stack(halves(np.where((sig == 0)[:, None], real_rows, imag_rows)))
    plain = np.concatenate([cos[:, :BLOCKS], -sin[:, :BLOCKS]], axis=0)
    high, low = halves(plain)
    plain_outer = np.concatenate([high, low, high], axis=1)
    plain_back = np.stack(halves(np.concatenate([cos[:BLOCKS], -sin[:BLOCKS]], axis=1)))
    return outer, twiddle, inner, back, plain_outer, plain_back


def split(value):
    high = value.astype(BF16)
    return high, (value - high.astype(F32)).astype(BF16)


def mul(left, right, rhs_minor=False):
    dims = (((1,), (1 if rhs_minor else 0,)), ((), ()))
    return lax.dot_general(left, right, dims, preferred_element_type=F32)


def times_table(value, table, rhs_minor=False):
    high, low = split(value)
    return (
        mul(high, table[0], rhs_minor) + mul(low, table[0], rhs_minor) + mul(high, table[1], rhs_minor)
    )


def table_times(table, value):
    high, low = split(value)
    return mul(table[0], high) + mul(table[0], low) + mul(table[1], high)


def inner_forward(first, twiddle, inner):
    tc, ts = twiddle[0], twiddle[1]
    rows = []
    for s in range(first.shape[0] // (2 * SIDE)):
        re = first[2 * s * SIDE:(2 * s + 1) * SIDE]
        im = first[(2 * s + 1) * SIDE:(2 * s + 2) * SIDE]
        rows.append(jnp.concatenate([re * tc + im * ts, im * tc - re * ts], axis=1))
    stacked = rows[0] if len(rows) == 1 else jnp.concatenate(rows, axis=0)
    return times_table(stacked, inner)


def inner_backward(spec, twiddle, inner):
    tc, ts = twiddle[0], twiddle[1]
    mid = times_table(spec, inner, rhs_minor=True)
    re, im = mid[:, :SIDE], mid[:, SIDE:]
    return jnp.concatenate([re * tc - im * ts, im * tc + re * ts], axis=0)


def taps_spectrum(taps, plain_outer, twiddle, inner):
    scale = 1.0 / (math.sqrt(LENGTH) * SIDE * SIDE)
    high, low = split(taps * scale)
    first = mul(plain_outer, jnp.concatenate([high, high, low], axis=0))
    return inner_forward(first, twiddle, inner)


def project_kernel(*refs):
    sources, (send_ref, spec_ref, twiddle, inner, weights) = refs[:6], refs[6:11]
    plain_outer, taps, tokens, sems = refs[11:]
    held = (plain_outer, twiddle, inner, taps, tokens, weights)
    copies = [
        pltpu.make_async_copy(source, target, sems.at[i])
        for i, (source, target) in enumerate(zip(sources[:5], held[:5]))
    ] + [
        pltpu.make_async_copy(sources[5].at[s], weights.at[s], sems.at[5 + s]) for s in range(3)
    ]
    for copy in copies:
        copy.start()
    for copy in copies[:4]:
        copy.wait()
    spec_ref[...] = taps_spectrum(taps[...], plain_outer[...], twiddle, inner)
    copies[4].wait()
    for s in range(3):
        copies[5 + s].wait()
        part = mul(tokens[...], weights[s]).T.astype(BF16)
        for k, g in enumerate(CH_ORDER):
            send_ref[k, s] = part[GROUP * g:GROUP * (g + 1)]


def swap_peers(rows_ref):
    far = pl.ds(2 * CTX_FIRST, 2)
    first, other = rows_ref[0:2], rows_ref[far]
    rows_ref[0:2] = other
    rows_ref[far] = first


def gate_kernel(parts_ref, cotangent_ref, fields_ref, send_ref, scratch):
    fields = []
    for s in range(3):
        total = parts_ref[0, s].astype(F32)
        for g in range(1, CH):
            total = total + parts_ref[g, s].astype(F32)
        rounded = total.astype(BF16)
        fields_ref[s] = rounded
        fields.append(rounded.astype(F32))
    scratch[pl.ds(0, CTX, stride=2), :] = fields[1] * fields[2]
    scratch[pl.ds(1, CTX, stride=2), :] = cotangent_ref[...].astype(F32) * fields[0]
    swap_peers(scratch)
    send_ref[...] = scratch[...].astype(BF16)


def conv_kernel(rows_ref, taps_ref, outer_ref, twiddle_ref, inner_ref, back_ref, spec_ref, send_ref):
    rows = rows_ref[...]
    first = mul(outer_ref[...], jnp.concatenate([rows, rows], axis=0))
    spec = inner_forward(first, twiddle_ref, inner_ref)
    spec_ref[...] = spec
    pr, pi = spec[:SIDE, :SIDE], spec[:SIDE, SIDE:]
    gr, gi = spec[SIDE:, :SIDE], spec[SIDE:, SIDE:]
    kr, ki = taps_ref[:, :SIDE], taps_ref[:, SIDE:]
    re = pr * kr - pi * ki - (gi * kr - gr * ki)
    im = pr * ki + pi * kr + (gr * kr + gi * ki)
    mid = inner_backward(jnp.concatenate([re, im], axis=1), twiddle_ref, inner_ref)
    send_ref[...] = table_times(back_ref, mid).astype(BF16)


def filter_grad(spec_ref, twiddle_ref, inner_ref, plain_back_ref):
    scale = 1.0 / (math.sqrt(LENGTH) * SIDE * SIDE)
    pr, pi = spec_ref[:SIDE, :SIDE], spec_ref[:SIDE, SIDE:]
    gr, gi = spec_ref[SIDE:, :SIDE], spec_ref[SIDE:, SIDE:]
    re = (gr * pr + gi * pi) * scale
    im = (gi * pr - gr * pi) * scale
    mid = inner_backward(jnp.concatenate([re, im], axis=1), twiddle_ref, inner_ref)
    return table_times(plain_back_ref, mid)


def finish_kernel(
    grads_ref, gated_in_ref, weights_ref, spec_ref, twiddle_ref, inner_ref, plain_back_ref,
    gated_ref, input_ref, filter_ref,
):
    gated_ref[...] = gated_in_ref[...]
    filter_ref[...] = filter_grad(spec_ref, twiddle_ref, inner_ref, plain_back_ref)
    total = None
    for s in range(3):
        rows = jnp.concatenate([grads_ref[CH_ORDER.index(g), s] for g in range(CH)], axis=0)
        part = mul(rows.T, weights_ref[s], rhs_minor=True)
        total = part if total is None else total + part
    input_ref[...] = total.astype(BF16)


def grads_kernel(rows_ref, fields_ref, cotangent_ref, send_ref, gated_ref, scratch):
    scratch[...] = rows_ref[...].astype(F32)
    swap_peers(scratch)
    convolved = scratch[pl.ds(0, CTX, stride=2), :]
    prod_grad = scratch[pl.ds(1, CTX, stride=2), :]
    query, key, value = (fields_ref[s].astype(F32) for s in range(3))
    upstream = cotangent_ref[...].astype(F32)
    gated_ref[...] = (query * convolved).astype(BF16)
    for s, row in enumerate((upstream * convolved, prod_grad * value, prod_grad * key)):
        row = row.astype(BF16)
        for k in range(CH):
            send_ref[k, s] = row


def call(kernel, shapes, scratch=(), params=SMALL, **extra):
    return pl.pallas_call(
        kernel, out_shape=shapes, compiler_params=params, scratch_shapes=list(scratch), **extra
    )


def shape(dims, dtype):
    return jax.ShapeDtypeStruct(dims, dtype)


def exchange(field, axis, order):
    return lax.all_to_all(
        field, axis, split_axis=0, concat_axis=0, tiled=True, axis_index_groups=[list(order)]
    )


def over_ctx(rows):
    return exchange(rows.reshape(CTX, 2, SIDE), "ctx", CTX_ORDER).reshape(SIDE, SIDE)


def on_device(tokens, weights, filter_taps, cotangent):
    outer, twiddle, inner, back, plain_outer, plain_back = (jnp.asarray(t) for t in make_tables())
    message = (CH, 3, GROUP, SIDE)
    operands = (plain_outer, twiddle, inner, filter_taps.reshape(BLOCKS, SIDE), tokens, weights)
    kept = (twiddle, inner, weights)
    parts, taps_spec, twiddle, inner, weights = call(
        project_kernel,
        (pltpu.VMEM(message, BF16), pltpu.VMEM((SIDE, 2 * SIDE), F32))
        + tuple(pltpu.VMEM(t.shape, t.dtype) for t in kept),
        [pltpu.VMEM(operands[i].shape, operands[i].dtype) for i in (0, 3, 4)]
        + [pltpu.SemaphoreType.DMA((8,))],
        LARGE,
        in_specs=[pl.BlockSpec(memory_space=pltpu.HBM)] * 6,
    )(*(pltpu.with_memory_space_constraint(t, pltpu.HBM) for t in operands))
    parts = exchange(parts, "ch", CH_ORDER)
    fields, send = call(
        gate_kernel,
        (shape((3, GROUP, SIDE), BF16), shape((SIDE, SIDE), BF16)),
        [pltpu.VMEM((SIDE, SIDE), F32)],
    )(parts, cotangent)
    spec, send = call(
        conv_kernel, (shape((2 * SIDE, 2 * SIDE), F32), shape((SIDE, SIDE), BF16))
    )(over_ctx(send), taps_spec, outer, twiddle, inner, back)
    grads, gated = call(
        grads_kernel,
        (shape(message, BF16), shape((GROUP, SIDE), BF16)),
        [pltpu.VMEM((SIDE, SIDE), F32)],
    )(over_ctx(send), fields, cotangent)
    grads = exchange(grads, "ch", CH_ORDER)
    gated_out, input_grad, kernel_grad = call(
        finish_kernel,
        (
            shape((GROUP, SIDE), BF16),
            shape(tokens.shape, BF16),
            shape((BLOCKS, SIDE), F32),
        ),
    )(grads, gated, weights, spec, twiddle, inner, plain_back)
    return gated_out, input_grad, kernel_grad.reshape(1, 1, LENGTH)


def solution(mesh):
    return jax.shard_map(
        on_device,
        mesh=mesh,
        in_specs=(P("ctx", "ch"), P(None, "ch", None), P("ctx", "ch", None), P("ch", "ctx")),
        out_specs=(P("ch", "ctx"), P("ctx", "ch"), P("ctx", "ch", None)),
        check_vma=False,
    )
```

time: 83.9 us -> 73.4 us (0.87); the launches traced: 82.6 us -> 73.1 us
  blocking collectives: 75.6 us -> 66.2 us
    all_to_all x4, blocking collectives: 75.6 us -> 66.2 us  [exchange(): lax.all_to_all(field, axis, split_axis=0, concat_axis=0, tiled=True, axis...]
where the time goes in v3:
time: 73.4 us; the launch traced here: 73.1 us
  blocking collectives  66.2 us (90%)
  Pallas kernels  6.2 us (8%)
    all_to_all x4, blocking collectives, exchange(): lax.all_to_all(field, axis, split_axis=0, concat_axis=0, tiled=True, axis...  66.2 us
    pallas_call x1, Pallas kernels, on_device(): call(project_kernel, (pltpu.VMEM(message, BF16), pltpu.VMEM((SIDE, 2 * SI...  2.85 us
    pallas_call x1, Pallas kernels, on_device(): call(finish_kernel, (shape((GROUP, SIDE), BF16), shape(tokens.shape, BF16...  2.21 us

profile of v3, /device:TPU:24, one launch (start us, length us, event | category | flops | bytes accessed | tf_op | source)
XLA Modules:
  0.0 73.1 jit_solution(10005413367699656982)
XLA Ops:
  0.6 0.0 copy-start.1
  0.6 0.0 copy-start
  0.7 0.0 copy-start.3
  0.7 0.0 copy-start.2
  0.7 2.8 %shard_map.121 = (bf16[8,3,64,128]{3,2,1,0:T(8,128)(2,1)S(1)}, f32[128,256]{1,0:T(8,128)S(1)}, f32[2,128,128]{2,1,0:T(8,128)S(1)}, bf16[2,256,256]{2,1,0:T(8,128)(2,1)S(1)}, bf16[3,1024,512]{2,1,0:T(8,128)(2,1)S(1)}) custom-call(bf16[256,192]{1,0:T(8,128)(2,1)} %constant.16.clone.refs_0_, f32[2,128,128]{2,1,0:T(8,128)} %constant.13.clone.refs_1_, ...), custom_call_target="tpu_custom_call" | custom-call | tf_op jit(solution)/shard_map/pallas_call | solution.py:229
  3.5 12.2 %all_to_all.20.parts_ref = bf16[8,3,64,128]{3,2,1,0:T(8,128)(2,1)S(1)} all-to-all(bf16[8,3,64,128]{3,2,1,0:T(8,128)(2,1)S(1)} %get-tuple-element.17), channel_id=1, replica_groups={{7,1,2,3,4,5,6,0},{15,9,10,11,12,13,14,8},{23,17,18,19,20,21,22,16},{31..., dimensions={0} | all-to-all | bytes 786432 | tf_op jit(solution)/shard_map/all_to_all | solution.py:215
  15.7 0.0 copy-done.3
  15.7 0.1 shard_map.122
  15.8 24.9 %all_to_all.21 = bf16[64,2,128]{2,1,0:T(2,128)(2,1)S(1)} all-to-all(bf16[64,2,128]{2,1,0:T(2,128)(2,1)S(1)} %bitcast.9), channel_id=1, replica_groups={{432,8,16,24,32,40,48,56,64,72,80,88,96,104,112,120,128,136,144,152,160..., dimensions={0} | all-to-all | bytes 65536 | tf_op jit(solution)/shard_map/all_to_all | solution.py:215
  40.6 0.0 copy-done.1
  40.6 0.0 copy-done
  40.6 1.0 %shard_map.123 = (f32[256,256]{1,0:T(8,128)S(1)}, bf16[128,128]{1,0:T(8,128)(2,1)S(1)}) custom-call(bf16[128,128]{1,0:T(8,128)(2,1)S(1)} %bitcast.7, f32[128,256]{1,0:T(8,128)S(1)} %get-tuple-element.19.taps_ref, bf16[512,256]{1,0:T(8,128)(2,1)S(1)} %copy-done, f32[2,128,128]{2,1,0:T(8,128)S(1)} %get-tuple-element.20.twiddle_ref, ...), custom_call_target="tpu_custom_call" | custom-call | tf_op jit(solution)/shard_map/pallas_call | solution.py:244
  41.7 17.9 %all_to_all.22 = bf16[64,2,128]{2,1,0:T(2,128)(2,1)S(1)} all-to-all(bf16[64,2,128]{2,1,0:T(2,128)(2,1)S(1)} %bitcast.8), channel_id=1, replica_groups={{432,8,16,24,32,40,48,56,64,72,80,88,96,104,112,120,128,136,144,152,160..., dimensions={0} | all-to-all | bytes 65536 | tf_op jit(solution)/shard_map/all_to_all | solution.py:215
  59.6 11.3 %all_to_all.23.grads_ref = bf16[8,3,64,128]{3,2,1,0:T(8,128)(2,1)S(1)} all-to-all(bf16[8,3,64,128]{3,2,1,0:T(8,128)(2,1)S(1)} %get-tuple-element.24), channel_id=1, replica_groups={{7,1,2,3,4,5,6,0},{15,9,10,11,12,13,14,8},{23,17,18,19,20,21,22,16},{31..., dimensions={0} | all-to-all | bytes 786432 | tf_op jit(solution)/shard_map/all_to_all | solution.py:215
  70.9 0.0 copy-done.2
  70.9 2.2 %shard_map.125 = (bf16[64,128]{1,0:T(8,128)(2,1)}, bf16[128,1024]{1,0:T(8,128)(2,1)}, f32[64,128]{1,0:T(8,128)}) custom-call(bf16[8,3,64,128]{3,2,1,0:T(8,128)(2,1)S(1)} %all_to_all.23.grads_ref, bf16[64,128]{1,0:T(8,128)(2,1)S(1)} %get-tuple-element.25.gated_in_ref, bf16[3,1024,512]{2,1,0:T(8,128)(2,1)S(1)} %get-tuple-element.26.weights_ref, ...), custom_call_target="tpu_custom_call" | custom-call | tf_op jit(solution)/shard_map/pallas_call | solution.py:253
  (1 shorter events, 0.0 us)
Async XLA Ops:
  0.6 40.0 %copy-start.1 = (bf16[2,128,256]{2,1,0:T(8,128)(2,1)S(1)}, bf16[2,128,256]{2,1,0:T(8,128)(2,1)}, u32[]{:S(2)}) copy-start(bf16[2,128,256]{2,1,0:T(8,128)(2,1)} %constant.15.clone.back_ref) | copy-start | bytes 393220
  0.6 40.0 %copy-start = (bf16[512,256]{1,0:T(8,128)(2,1)S(1)}, bf16[512,256]{1,0:T(8,128)(2,1)}, u32[]{:S(2)}) copy-start(bf16[512,256]{1,0:T(8,128)(2,1)} %constant.12.clone.outer_ref) | copy-start | bytes 786436
  0.7 15.0 %copy-start.3 = (bf16[64,128]{1,0:T(8,128)(2,1)S(1)}, bf16[64,128]{1,0:T(8,128)(2,1)}, u32[]{:S(2)}) copy-start(bf16[64,128]{1,0:T(8,128)(2,1)} %cotangent_ref.3) | copy-start | bytes 49156
  0.7 70.2 %copy-start.2 = (bf16[2,64,256]{2,1,0:T(8,128)(2,1)S(1)}, bf16[2,64,256]{2,1,0:T(8,128)(2,1)}, u32[]{:S(2)}) copy-start(bf16[2,64,256]{2,1,0:T(8,128)(2,1)} %constant.17.clone.plain_back_ref) | copy-start | bytes 196612

commit v4 on v3

--- a/solution.py
+++ b/solution.py
@@ -90,41 +90,35 @@
     return times_table(stacked, inner)
 
 
-def inner_backward(spec, twiddle, inner):
+def turn_back(mid, twiddle):
     tc, ts = twiddle[0], twiddle[1]
-    mid = times_table(spec, inner, rhs_minor=True)
     re, im = mid[:, :SIDE], mid[:, SIDE:]
     return jnp.concatenate([re * tc - im * ts, im * tc + re * ts], axis=0)
 
 
-def taps_spectrum(taps, plain_outer, twiddle, inner):
-    scale = 1.0 / (math.sqrt(LENGTH) * SIDE * SIDE)
-    high, low = split(taps * scale)
-    first = mul(plain_outer, jnp.concatenate([high, high, low], axis=0))
-    return inner_forward(first, twiddle, inner)
-
-
-def project_kernel(*refs):
-    sources, (send_ref, spec_ref, twiddle, inner, weights) = refs[:6], refs[6:11]
-    plain_outer, taps, tokens, sems = refs[11:]
-    held = (plain_outer, twiddle, inner, taps, tokens, weights)
-    copies = [
-        pltpu.make_async_copy(source, target, sems.at[i])
-        for i, (source, target) in enumerate(zip(sources[:5], held[:5]))
-    ] + [
-        pltpu.make_async_copy(sources[5].at[s], weights.at[s], sems.at[5 + s]) for s in range(3)
+def project_kernel(tokens_hbm, weights_hbm, send_ref, weights, tokens, sems):
+    half = weights.shape[1] // 2
+    parts = [pl.ds(h * half, half) for h in range(2)]
+    tokens_copy = pltpu.make_async_copy(tokens_hbm, tokens, sems.at[6])
+    tokens_copy.start()
+    blocks = [
+        pltpu.make_async_copy(
+            weights_hbm.at[i // 2, parts[i % 2]], weights.at[i // 2, parts[i % 2]], sems.at[i]
+        )
+        for i in range(6)
     ]
-    for copy in copies:
+    for copy in blocks:
         copy.start()
-    for copy in copies[:4]:
-        copy.wait()
-    spec_ref[...] = taps_spectrum(taps[...], plain_outer[...], twiddle, inner)
-    copies[4].wait()
+    tokens_copy.wait()
     for s in range(3):
-        copies[5 + s].wait()
-        part = mul(tokens[...], weights[s]).T.astype(BF16)
+        total = None
+        for h in range(2):
+            blocks[2 * s + h].wait()
+            part = mul(tokens[:, half * h:half * (h + 1)], weights[s, half * h:half * (h + 1)])
+            total = part if total is None else total + part
+        total = total.astype(BF16).T
         for k, g in enumerate(CH_ORDER):
-            send_ref[k, s] = part[GROUP * g:GROUP * (g + 1)]
+            send_ref[k, s] = total[GROUP * g:GROUP * (g + 1)]
 
 
 def swap_peers(rows_ref):
@@ -149,42 +143,47 @@
     send_ref[...] = scratch[...].astype(BF16)
 
 
-def conv_kernel(rows_ref, taps_ref, outer_ref, twiddle_ref, inner_ref, back_ref, spec_ref, send_ref):
+def conv_kernel(
+    rows_ref, taps_ref, outer_ref, plain_outer_ref, twiddle_ref, inner_ref, back_ref,
+    plain_back_ref, filter_ref, send_ref,
+):
     rows = rows_ref[...]
+    high, low = split(taps_ref[...] * (1.0 / (math.sqrt(LENGTH) * SIDE * SIDE)))
+    taps = mul(plain_outer_ref[...], jnp.concatenate([high, high, low], axis=0))
     first = mul(outer_ref[...], jnp.concatenate([rows, rows], axis=0))
-    spec = inner_forward(first, twiddle_ref, inner_ref)
-    spec_ref[...] = spec
-    pr, pi = spec[:SIDE, :SIDE], spec[:SIDE, SIDE:]
-    gr, gi = spec[SIDE:, :SIDE], spec[SIDE:, SIDE:]
-    kr, ki = taps_ref[:, :SIDE], taps_ref[:, SIDE:]
+    spec = inner_forward(jnp.concatenate([first, taps], axis=0), twiddle_ref, inner_ref)
+    (pr, pi), (gr, gi), (kr, ki) = (
+        (spec[s * SIDE:(s + 1) * SIDE, :SIDE], spec[s * SIDE:(s + 1) * SIDE, SIDE:])
+        for s in range(3)
+    )
     re = pr * kr - pi * ki - (gi * kr - gr * ki)
     im = pr * ki + pi * kr + (gr * kr + gi * ki)
-    mid = inner_backward(jnp.concatenate([re, im], axis=1), twiddle_ref, inner_ref)
-    send_ref[...] = table_times(back_ref, mid).astype(BF16)
-
-
-def filter_grad(spec_ref, twiddle_ref, inner_ref, plain_back_ref):
     scale = 1.0 / (math.sqrt(LENGTH) * SIDE * SIDE)
-    pr, pi = spec_ref[:SIDE, :SIDE], spec_ref[:SIDE, SIDE:]
-    gr, gi = spec_ref[SIDE:, :SIDE], spec_ref[SIDE:, SIDE:]
-    re = (gr * pr + gi * pi) * scale
-    im = (gi * pr - gr * pi) * scale
-    mid = inner_backward(jnp.concatenate([re, im], axis=1), twiddle_ref, inner_ref)
-    return table_times(plain_back_ref, mid)
+    filter_re = (gr * pr + gi * pi) * scale
+    filter_im = (gi * pr - gr * pi) * scale
+    both = jnp.concatenate(
+        [
+            jnp.concatenate([re, im], axis=1),
+            jnp.concatenate([filter_re, filter_im], axis=1),
+        ],
+        axis=0,
+    )
+    mid = times_table(both, inner_ref, rhs_minor=True)
+    send_ref[...] = table_times(back_ref, turn_back(mid[:SIDE], twiddle_ref)).astype(BF16)
+    filter_ref[...] = table_times(plain_back_ref, turn_back(mid[SIDE:], twiddle_ref))
 
 
 def finish_kernel(
-    grads_ref, gated_in_ref, weights_ref, spec_ref, twiddle_ref, inner_ref, plain_back_ref,
-    gated_ref, input_ref, filter_ref,
+    grads_ref, gated_in_ref, filter_in_ref, weights_ref, gated_ref, input_ref, filter_ref
 ):
     gated_ref[...] = gated_in_ref[...]
-    filter_ref[...] = filter_grad(spec_ref, twiddle_ref, inner_ref, plain_back_ref)
+    filter_ref[...] = filter_in_ref[...]
     total = None
     for s in range(3):
         rows = jnp.concatenate([grads_ref[CH_ORDER.index(g), s] for g in range(CH)], axis=0)
-        part = mul(rows.T, weights_ref[s], rhs_minor=True)
+        part = mul(weights_ref[s], rows)
         total = part if total is None else total + part
-    input_ref[...] = total.astype(BF16)
+    input_ref[...] = total.astype(BF16).T
 
 
 def grads_kernel(rows_ref, fields_ref, cotangent_ref, send_ref, gated_ref, scratch):
@@ -222,28 +221,27 @@
 
 
 def on_device(tokens, weights, filter_taps, cotangent):
-    outer, twiddle, inner, back, plain_outer, plain_back = (jnp.asarray(t) for t in make_tables())
+    tables = [jnp.asarray(t) for t in make_tables()]
     message = (CH, 3, GROUP, SIDE)
-    operands = (plain_outer, twiddle, inner, filter_taps.reshape(BLOCKS, SIDE), tokens, weights)
-    kept = (twiddle, inner, weights)
-    parts, taps_spec, twiddle, inner, weights = call(
+    parts, weights = call(
         project_kernel,
-        (pltpu.VMEM(message, BF16), pltpu.VMEM((SIDE, 2 * SIDE), F32))
-        + tuple(pltpu.VMEM(t.shape, t.dtype) for t in kept),
-        [pltpu.VMEM(operands[i].shape, operands[i].dtype) for i in (0, 3, 4)]
-        + [pltpu.SemaphoreType.DMA((8,))],
+        (pltpu.VMEM(message, BF16), pltpu.VMEM(weights.shape, BF16)),
+        [pltpu.VMEM(tokens.shape, BF16), pltpu.SemaphoreType.DMA((7,))],
         LARGE,
-        in_specs=[pl.BlockSpec(memory_space=pltpu.HBM)] * 6,
-    )(*(pltpu.with_memory_space_constraint(t, pltpu.HBM) for t in operands))
+        in_specs=[pl.BlockSpec(memory_space=pltpu.HBM)] * 2,
+    )(*(pltpu.with_memory_space_constraint(t, pltpu.HBM) for t in (tokens, weights)))
+    taps = filter_taps.reshape(BLOCKS, SIDE)
+    parts, taps, cotangent, *tables = lax.optimization_barrier((parts, taps, cotangent, *tables))
+    outer, twiddle, inner, back, plain_outer, plain_back = tables
     parts = exchange(parts, "ch", CH_ORDER)
     fields, send = call(
         gate_kernel,
         (shape((3, GROUP, SIDE), BF16), shape((SIDE, SIDE), BF16)),
         [pltpu.VMEM((SIDE, SIDE), F32)],
     )(parts, cotangent)
-    spec, send = call(
-        conv_kernel, (shape((2 * SIDE, 2 * SIDE), F32), shape((SIDE, SIDE), BF16))
-    )(over_ctx(send), taps_spec, outer, twiddle, inner, back)
+    kernel_grad, send = call(
+        conv_kernel, (shape((BLOCKS, SIDE), F32), shape((SIDE, SIDE), BF16))
+    )(over_ctx(send), taps, outer, plain_outer, twiddle, inner, back, plain_back)
     grads, gated = call(
         grads_kernel,
         (shape(message, BF16), shape((GROUP, SIDE), BF16)),
@@ -257,7 +255,7 @@
             shape(tokens.shape, BF16),
             shape((BLOCKS, SIDE), F32),
         ),
-    )(grads, gated, weights, spec, twiddle, inner, plain_back)
+    )(grads, gated, kernel_grad, weights)
     return gated_out, input_grad, kernel_grad.reshape(1, 1, LENGTH)
 
 

time: 73.4 us -> 72.9 us (level)
  no operation moved by 1% of the time
where the time goes in v4:
time: 72.9 us; the launch traced here: 72.7 us
  blocking collectives  66.2 us (91%)
  Pallas kernels  5.71 us (8%)
  between operations  0.75 us (1%)
    all_to_all x4, blocking collectives, exchange(): lax.all_to_all(field, axis, split_axis=0, concat_axis=0, tiled=True, axis...  66.2 us
    pallas_call x1, Pallas kernels, on_device(): call(project_kernel, (pltpu.VMEM(message, BF16), pltpu.VMEM(weights.shape...  2.69 us
    pallas_call x1, Pallas kernels, on_device(): call(finish_kernel, (shape((GROUP, SIDE), BF16), shape(tokens.shape, BF16...  1.73 us

profile of v4, /device:TPU:24, one launch (start us, length us, event | category | flops | bytes accessed | tf_op | source)
XLA Modules:
  0.0 72.7 jit_solution(3020396054591443792)
XLA Ops:
  0.6 0.0 copy-start.5
  0.6 0.0 copy-start.2
  0.7 0.0 copy-start.3
  0.7 0.0 copy-start
  0.7 0.0 copy-start.4
  0.7 0.0 copy-start.1
  0.7 0.0 copy-start.6
  0.7 0.0 copy-start.7
  0.7 2.7 %shard_map.121 = (bf16[8,3,64,128]{3,2,1,0:T(8,128)(2,1)S(1)}, bf16[3,1024,512]{2,1,0:T(8,128)(2,1)S(1)}) custom-call(bf16[128,1024]{1,0:T(8,128)(2,1)} %tokens_hbm.1, bf16[3,1024,512]{2,1,0:T(8,128)(2,1)} %weights_hbm.1), custom_call_target="tpu_custom_call" | custom-call | tf_op jit(solution)/shard_map/pallas_call | solution.py:226
  3.4 12.1 %all_to_all.20.parts_ref = bf16[8,3,64,128]{3,2,1,0:T(8,128)(2,1)S(1)} all-to-all(bf16[8,3,64,128]{3,2,1,0:T(8,128)(2,1)S(1)} %get-tuple-element.24), channel_id=1, replica_groups={{7,1,2,3,4,5,6,0},{15,9,10,11,12,13,14,8},{23,17,18,19,20,21,22,16},{31..., dimensions={0} | all-to-all | bytes 786432 | tf_op jit(solution)/shard_map/all_to_all | solution.py:214
  15.6 0.0 copy-done.6
  15.6 0.1 shard_map.122
  15.6 24.9 %all_to_all.21 = bf16[64,2,128]{2,1,0:T(2,128)(2,1)S(1)} all-to-all(bf16[64,2,128]{2,1,0:T(2,128)(2,1)S(1)} %bitcast.10), channel_id=1, replica_groups={{432,8,16,24,32,40,48,56,64,72,80,88,96,104,112,120,128,136,144,152,160..., dimensions={0} | all-to-all | bytes 65536 | tf_op jit(solution)/shard_map/all_to_all | solution.py:214
  40.5 0.0 copy-done.5
  40.5 0.0 copy-done.2
  40.5 0.0 copy-done.3
  40.5 0.0 copy-done
  40.5 0.0 copy-done.4
  40.5 0.0 copy-done.1
  40.6 0.0 copy-done.7
  40.6 1.2 %shard_map.123 = (f32[64,128]{1,0:T(8,128)S(1)}, bf16[128,128]{1,0:T(8,128)(2,1)S(1)}) custom-call(bf16[128,128]{1,0:T(8,128)(2,1)S(1)} %bitcast.6, f32[64,128]{1,0:T(8,128)S(1)} %bitcast.8, bf16[512,256]{1,0:T(8,128)(2,1)S(1)} %copy-done.1, bf16[256,192]{1,0:T(8,128)(2,1)S(1)} %copy-done.2, f32[2,128,128]{2,1,0:T(8,128)S(1)} %copy-done.4, ...), custom_call_target="tpu_custom_call" | custom-call | tf_op jit(solution)/shard_map/pallas_call | solution.py:242
  41.7 17.9 %all_to_all.22 = bf16[64,2,128]{2,1,0:T(2,128)(2,1)S(1)} all-to-all(bf16[64,2,128]{2,1,0:T(2,128)(2,1)S(1)} %bitcast.9), channel_id=1, replica_groups={{432,8,16,24,32,40,48,56,64,72,80,88,96,104,112,120,128,136,144,152,160..., dimensions={0} | all-to-all | bytes 65536 | tf_op jit(solution)/shard_map/all_to_all | solution.py:214
  59.7 11.3 %all_to_all.23.grads_ref = bf16[8,3,64,128]{3,2,1,0:T(8,128)(2,1)S(1)} all-to-all(bf16[8,3,64,128]{3,2,1,0:T(8,128)(2,1)S(1)} %get-tuple-element.36), channel_id=1, replica_groups={{7,1,2,3,4,5,6,0},{15,9,10,11,12,13,14,8},{23,17,18,19,20,21,22,16},{31..., dimensions={0} | all-to-all | bytes 786432 | tf_op jit(solution)/shard_map/all_to_all | solution.py:214
  71.0 1.7 %shard_map.125 = (bf16[64,128]{1,0:T(8,128)(2,1)}, bf16[128,1024]{1,0:T(8,128)(2,1)}, f32[64,128]{1,0:T(8,128)}) custom-call(bf16[8,3,64,128]{3,2,1,0:T(8,128)(2,1)S(1)} %all_to_all.23.grads_ref, bf16[64,128]{1,0:T(8,128)(2,1)S(1)} %get-tuple-element.37.gated_in_ref, f32[64,128]{1,0:T(8,128)S(1)} %get-tuple-element.38.filter_in_ref, ...), custom_call_target="tpu_custom_call" | custom-call | tf_op jit(solution)/shard_map/pallas_call | solution.py:251
  (1 shorter events, 0.0 us)
Async XLA Ops:
  0.6 39.9 %copy-start.5 = (bf16[2,64,256]{2,1,0:T(8,128)(2,1)S(1)}, bf16[2,64,256]{2,1,0:T(8,128)(2,1)}, u32[]{:S(2)}) copy-start(bf16[2,64,256]{2,1,0:T(8,128)(2,1)} %constant.17.clone.plain_back_ref) | copy-start | bytes 196612
  0.6 39.9 %copy-start.2 = (bf16[256,192]{1,0:T(8,128)(2,1)S(1)}, bf16[256,192]{1,0:T(8,128)(2,1)}, u32[]{:S(2)}) copy-start(bf16[256,192]{1,0:T(8,128)(2,1)} %constant.16.clone.plain_outer_ref) | copy-start | bytes 294916
  0.7 39.9 %copy-start.3 = (bf16[2,128,256]{2,1,0:T(8,128)(2,1)S(1)}, bf16[2,128,256]{2,1,0:T(8,128)(2,1)}, u32[]{:S(2)}) copy-start(bf16[2,128,256]{2,1,0:T(8,128)(2,1)} %constant.15.clone.back_ref) | copy-start | bytes 393220
  0.7 39.9 %copy-start = (bf16[2,256,256]{2,1,0:T(8,128)(2,1)S(1)}, bf16[2,256,256]{2,1,0:T(8,128)(2,1)}, u32[]{:S(2)}) copy-start(bf16[2,256,256]{2,1,0:T(8,128)(2,1)} %constant.14.clone.inner_ref) | copy-start | bytes 786436
  0.7 39.9 %copy-start.4 = (f32[2,128,128]{2,1,0:T(8,128)S(1)}, f32[2,128,128]{2,1,0:T(8,128)}, u32[]{:S(2)}) copy-start(f32[2,128,128]{2,1,0:T(8,128)} %constant.13.clone.twiddle_ref) | copy-start | bytes 393220
  0.7 39.9 %copy-start.1 = (bf16[512,256]{1,0:T(8,128)(2,1)S(1)}, bf16[512,256]{1,0:T(8,128)(2,1)}, u32[]{:S(2)}) copy-start(bf16[512,256]{1,0:T(8,128)(2,1)} %constant.12.clone.outer_ref) | copy-start | bytes 786436
  0.7 14.9 %copy-start.6 = (bf16[64,128]{1,0:T(8,128)(2,1)S(1)}, bf16[64,128]{1,0:T(8,128)(2,1)}, u32[]{:S(2)}) copy-start(bf16[64,128]{1,0:T(8,128)(2,1)} %cotangent_ref.1) | copy-start | bytes 49156
  0.7 39.8 %copy-start.7 = (f32[1,1,8192]{2,1,0:T(1,128)S(1)}, f32[1,1,8192]{2,1,0:T(1,128)}, u32[]{:S(2)}) copy-start(f32[1,1,8192]{2,1,0:T(1,128)} %param.12) | copy-start | bytes 98308

commit v5 on v4

--- a/solution.py
+++ b/solution.py
@@ -23,7 +23,7 @@
     return order
 
 
-CTX_FIRST, CH_FIRST = 54, 7
+CTX_FIRST, CH_FIRST = 53, 7
 CTX_ORDER, CH_ORDER = led_by(CTX_FIRST, CTX), led_by(CH_FIRST, CH)
 LARGE = pltpu.CompilerParams(vmem_limit_bytes=20 * 1024 * 1024)
 SMALL = pltpu.CompilerParams(vmem_limit_bytes=8 * 1024 * 1024)
@@ -38,23 +38,10 @@
 def make_tables():
     index = np.arange(SIDE)
     angle = 2.0 * np.pi / SIDE * (np.outer(index, index) % SIDE)
-    cos, sin = np.cos(angle), np.sin(angle)
+    waves = np.stack(halves(np.cos(angle)) + halves(np.sin(angle)))
     turn = 2.0 * np.pi / (SIDE * SIDE) * np.outer(index, index)
     twiddle = np.stack([np.cos(turn), np.sin(turn)]).astype(np.float32)
-    block = np.repeat(np.array(CTX_ORDER), 2)
-    sig = np.tile(np.arange(2), CTX)
-    outer = np.concatenate([cos[:, block], -sin[:, block]], axis=0)
-    outer = np.concatenate([outer * (sig == 0), outer * (sig == 1)], axis=0)
-    outer = np.concatenate(halves(outer), axis=1)
-    inner = np.stack(halves(np.block([[cos, -sin], [sin, cos]])))
-    real_rows = np.concatenate([cos[block], -sin[block]], axis=1)
-    imag_rows = np.concatenate([sin[block], cos[block]], axis=1)
-    back = np.stack(halves(np.where((sig == 0)[:, None], real_rows, imag_rows)))
-    plain = np.concatenate([cos[:, :BLOCKS], -sin[:, :BLOCKS]], axis=0)
-    high, low = halves(plain)
-    plain_outer = np.concatenate([high, low, high], axis=1)
-    plain_back = np.stack(halves(np.concatenate([cos[:BLOCKS], -sin[:BLOCKS]], axis=1)))
-    return outer, twiddle, inner, back, plain_outer, plain_back
+    return waves, twiddle
 
 
 def split(value):
@@ -79,15 +66,8 @@
     return mul(table[0], high) + mul(table[0], low) + mul(table[1], high)
 
 
-def inner_forward(first, twiddle, inner):
-    tc, ts = twiddle[0], twiddle[1]
-    rows = []
-    for s in range(first.shape[0] // (2 * SIDE)):
-        re = first[2 * s * SIDE:(2 * s + 1) * SIDE]
-        im = first[(2 * s + 1) * SIDE:(2 * s + 2) * SIDE]
-        rows.append(jnp.concatenate([re * tc + im * ts, im * tc - re * ts], axis=1))
-    stacked = rows[0] if len(rows) == 1 else jnp.concatenate(rows, axis=0)
-    return times_table(stacked, inner)
+def block(rows):
+    return jnp.concatenate([jnp.concatenate(row, axis=1) for row in rows], axis=0)
 
 
 def turn_back(mid, twiddle):
@@ -143,15 +123,28 @@
     send_ref[...] = scratch[...].astype(BF16)
 
 
-def conv_kernel(
-    rows_ref, taps_ref, outer_ref, plain_outer_ref, twiddle_ref, inner_ref, back_ref,
-    plain_back_ref, filter_ref, send_ref,
-):
-    rows = rows_ref[...]
+def conv_kernel(rows_ref, taps_ref, waves_ref, twiddle_ref, filter_ref, send_ref, scratch):
+    cos, sin = (waves_ref[0], waves_ref[1]), (waves_ref[2], waves_ref[3])
+    tc, ts = twiddle_ref[0], twiddle_ref[1]
+    scratch[...] = rows_ref[...].astype(F32)
+    swap_peers(scratch)
+    product = scratch[pl.ds(0, CTX, stride=2), :].astype(BF16)
+    conv_grad = scratch[pl.ds(1, CTX, stride=2), :].astype(BF16)
     high, low = split(taps_ref[...] * (1.0 / (math.sqrt(LENGTH) * SIDE * SIDE)))
-    taps = mul(plain_outer_ref[...], jnp.concatenate([high, high, low], axis=0))
-    first = mul(outer_ref[...], jnp.concatenate([rows, rows], axis=0))
-    spec = inner_forward(jnp.concatenate([first, taps], axis=0), twiddle_ref, inner_ref)
+    signals = jnp.concatenate([product, conv_grad, high], axis=1)
+    signals = jnp.concatenate([signals, jnp.zeros_like(signals)], axis=0)
+    outer = [jnp.concatenate([cos[i], -sin[i]], axis=0) for i in range(2)]
+    first = mul(jnp.concatenate(outer, axis=1), jnp.concatenate([signals, signals], axis=0))
+    rest = mul(outer[0], jnp.concatenate([low, jnp.zeros_like(low)], axis=0))
+    turned = []
+    for s in range(3):
+        part = first[:, s * SIDE:(s + 1) * SIDE]
+        if s == 2:
+            part = part + rest
+        re, im = part[:SIDE], part[SIDE:]
+        turned.append(jnp.concatenate([re * tc + im * ts, im * tc - re * ts], axis=1))
+    inner = [block([[cos[i], -sin[i]], [sin[i], cos[i]]]) for i in range(2)]
+    spec = times_table(jnp.concatenate(turned, axis=0), inner)
     (pr, pi), (gr, gi), (kr, ki) = (
         (spec[s * SIDE:(s + 1) * SIDE, :SIDE], spec[s * SIDE:(s + 1) * SIDE, SIDE:])
         for s in range(3)
@@ -161,16 +154,19 @@
     scale = 1.0 / (math.sqrt(LENGTH) * SIDE * SIDE)
     filter_re = (gr * pr + gi * pi) * scale
     filter_im = (gi * pr - gr * pi) * scale
-    both = jnp.concatenate(
-        [
-            jnp.concatenate([re, im], axis=1),
-            jnp.concatenate([filter_re, filter_im], axis=1),
-        ],
-        axis=0,
-    )
-    mid = times_table(both, inner_ref, rhs_minor=True)
-    send_ref[...] = table_times(back_ref, turn_back(mid[:SIDE], twiddle_ref)).astype(BF16)
-    filter_ref[...] = table_times(plain_back_ref, turn_back(mid[SIDE:], twiddle_ref))
+    mid = times_table(block([[re, im], [filter_re, filter_im]]), inner, rhs_minor=True)
+    back = [
+        block([[cos[i][:BLOCKS], -sin[i][:BLOCKS]], [sin[i][:BLOCKS], cos[i][:BLOCKS]]])
+        for i in range(2)
+    ]
+    both = table_times(back, turn_back(mid[:SIDE], twiddle_ref))
+    scratch[pl.ds(0, CTX, stride=2), :] = both[:BLOCKS]
+    scratch[pl.ds(1, CTX, stride=2), :] = both[BLOCKS:]
+    swap_peers(scratch)
+    send_ref[...] = scratch[...].astype(BF16)
+    filter_ref[...] = table_times(
+        [part[:BLOCKS] for part in back], turn_back(mid[SIDE:], twiddle_ref)
+    )
 
 
 def finish_kernel(
@@ -221,7 +217,7 @@
 
 
 def on_device(tokens, weights, filter_taps, cotangent):
-    tables = [jnp.asarray(t) for t in make_tables()]
+    waves, twiddle = (jnp.asarray(t) for t in make_tables())
     message = (CH, 3, GROUP, SIDE)
     parts, weights = call(
         project_kernel,
@@ -230,9 +226,6 @@
         LARGE,
         in_specs=[pl.BlockSpec(memory_space=pltpu.HBM)] * 2,
     )(*(pltpu.with_memory_space_constraint(t, pltpu.HBM) for t in (tokens, weights)))
-    taps = filter_taps.reshape(BLOCKS, SIDE)
-    parts, taps, cotangent, *tables = lax.optimization_barrier((parts, taps, cotangent, *tables))
-    outer, twiddle, inner, back, plain_outer, plain_back = tables
     parts = exchange(parts, "ch", CH_ORDER)
     fields, send = call(
         gate_kernel,
@@ -240,8 +233,10 @@
         [pltpu.VMEM((SIDE, SIDE), F32)],
     )(parts, cotangent)
     kernel_grad, send = call(
-        conv_kernel, (shape((BLOCKS, SIDE), F32), shape((SIDE, SIDE), BF16))
-    )(over_ctx(send), taps, outer, plain_outer, twiddle, inner, back, plain_back)
+        conv_kernel,
+        (shape((BLOCKS, SIDE), F32), shape((SIDE, SIDE), BF16)),
+        [pltpu.VMEM((SIDE, SIDE), F32)],
+    )(over_ctx(send), filter_taps.reshape(BLOCKS, SIDE), waves, twiddle)
     grads, gated = call(
         grads_kernel,
         (shape(message, BF16), shape((GROUP, SIDE), BF16)),

time: 72.9 us -> 72 us (0.988)
  blocking collectives: 66.2 us -> 65.4 us
    all_to_all x4, blocking collectives: 66.2 us -> 65.4 us  [exchange(): lax.all_to_all(field, axis, split_axis=0, concat_axis=0, tiled=True, axis...]
where the time goes in v5:
time: 72 us; the launch traced here: 71.7 us
  blocking collectives  65.4 us (91%)
  Pallas kernels  5.63 us (8%)
    all_to_all x4, blocking collectives, exchange(): lax.all_to_all(field, axis, split_axis=0, concat_axis=0, tiled=True, axis...  65.4 us
    pallas_call x1, Pallas kernels, on_device(): call(project_kernel, (pltpu.VMEM(message, BF16), pltpu.VMEM(weights.shape...  2.64 us
    pallas_call x1, Pallas kernels, on_device(): call(finish_kernel, (shape((GROUP, SIDE), BF16), shape(tokens.shape, BF16...  1.73 us

profile of v5, /device:TPU:24, one launch (start us, length us, event | category | flops | bytes accessed | tf_op | source)
XLA Modules:
  0.0 71.7 jit_solution(1022635324454817870)
XLA Ops:
  0.6 0.0 copy-start
  0.6 0.0 copy-start.1
  0.7 0.0 copy-start.2
  0.7 0.0 copy-start.3
  0.7 2.6 %shard_map.85 = (bf16[8,3,64,128]{3,2,1,0:T(8,128)(2,1)S(1)}, bf16[3,1024,512]{2,1,0:T(8,128)(2,1)S(1)}) custom-call(bf16[128,1024]{1,0:T(8,128)(2,1)} %tokens_hbm.1, bf16[3,1024,512]{2,1,0:T(8,128)(2,1)} %weights_hbm.1), custom_call_target="tpu_custom_call" | custom-call | tf_op jit(solution)/shard_map/pallas_call | solution.py:222
  3.3 12.1 %all_to_all.20.parts_ref = bf16[8,3,64,128]{3,2,1,0:T(8,128)(2,1)S(1)} all-to-all(bf16[8,3,64,128]{3,2,1,0:T(8,128)(2,1)S(1)} %get-tuple-element.14), channel_id=1, replica_groups={{7,1,2,3,4,5,6,0},{15,9,10,11,12,13,14,8},{23,17,18,19,20,21,22,16},{31..., dimensions={0} | all-to-all | bytes 786432 | tf_op jit(solution)/shard_map/all_to_all | solution.py:210
  15.5 0.0 copy-done.2
  15.5 0.1 shard_map.86
  15.5 24.5 %all_to_all.21 = bf16[64,2,128]{2,1,0:T(2,128)(2,1)S(1)} all-to-all(bf16[64,2,128]{2,1,0:T(2,128)(2,1)S(1)} %bitcast.10), channel_id=1, replica_groups={{424,8,16,24,32,40,48,56,64,72,80,88,96,104,112,120,128,136,144,152,160..., dimensions={0} | all-to-all | bytes 65536 | tf_op jit(solution)/shard_map/all_to_all | solution.py:210
  40.0 0.0 copy-done
  40.0 0.0 copy-done.1
  40.0 0.0 copy-done.3
  40.0 1.1 %shard_map.87 = (f32[64,128]{1,0:T(8,128)S(1)}, bf16[128,128]{1,0:T(8,128)(2,1)S(1)}) custom-call(bf16[128,128]{1,0:T(8,128)(2,1)S(1)} %bitcast.6, f32[64,128]{1,0:T(8,128)S(1)} %bitcast.8, bf16[4,128,128]{2,1,0:T(8,128)(2,1)S(1)} %copy-done.1, f32[2,128,128]{2,1,0:T(8,128)S(1)} %copy-done), custom_call_target="tpu_custom_call" | custom-call | tf_op jit(solution)/shard_map/pallas_call | solution.py:235
  41.2 17.5 %all_to_all.22 = bf16[64,2,128]{2,1,0:T(2,128)(2,1)S(1)} all-to-all(bf16[64,2,128]{2,1,0:T(2,128)(2,1)S(1)} %bitcast.9), channel_id=1, replica_groups={{424,8,16,24,32,40,48,56,64,72,80,88,96,104,112,120,128,136,144,152,160..., dimensions={0} | all-to-all | bytes 65536 | tf_op jit(solution)/shard_map/all_to_all | solution.py:210
  58.7 11.3 %all_to_all.23.grads_ref = bf16[8,3,64,128]{3,2,1,0:T(8,128)(2,1)S(1)} all-to-all(bf16[8,3,64,128]{3,2,1,0:T(8,128)(2,1)S(1)} %get-tuple-element.18), channel_id=1, replica_groups={{7,1,2,3,4,5,6,0},{15,9,10,11,12,13,14,8},{23,17,18,19,20,21,22,16},{31..., dimensions={0} | all-to-all | bytes 786432 | tf_op jit(solution)/shard_map/all_to_all | solution.py:210
  70.0 1.7 %shard_map.89 = (bf16[64,128]{1,0:T(8,128)(2,1)}, bf16[128,1024]{1,0:T(8,128)(2,1)}, f32[64,128]{1,0:T(8,128)}) custom-call(bf16[8,3,64,128]{3,2,1,0:T(8,128)(2,1)S(1)} %all_to_all.23.grads_ref, bf16[64,128]{1,0:T(8,128)(2,1)S(1)} %get-tuple-element.19.gated_in_ref, f32[64,128]{1,0:T(8,128)S(1)} %get-tuple-element.20.filter_in_ref, ...), custom_call_target="tpu_custom_call" | custom-call | tf_op jit(solution)/shard_map/pallas_call | solution.py:246
  (1 shorter events, 0.0 us)
Async XLA Ops:
  0.6 39.4 %copy-start = (f32[2,128,128]{2,1,0:T(8,128)S(1)}, f32[2,128,128]{2,1,0:T(8,128)}, u32[]{:S(2)}) copy-start(f32[2,128,128]{2,1,0:T(8,128)} %constant.5.clone.twiddle_ref) | copy-start | bytes 393220
  0.6 39.4 %copy-start.1 = (bf16[4,128,128]{2,1,0:T(8,128)(2,1)S(1)}, bf16[4,128,128]{2,1,0:T(8,128)(2,1)}, u32[]{:S(2)}) copy-start(bf16[4,128,128]{2,1,0:T(8,128)(2,1)} %constant.4.clone.waves_ref) | copy-start | bytes 393220
  0.7 14.8 %copy-start.2 = (bf16[64,128]{1,0:T(8,128)(2,1)S(1)}, bf16[64,128]{1,0:T(8,128)(2,1)}, u32[]{:S(2)}) copy-start(bf16[64,128]{1,0:T(8,128)(2,1)} %cotangent_ref.3) | copy-start | bytes 49156
  0.7 39.4 %copy-start.3 = (f32[1,1,8192]{2,1,0:T(1,128)S(1)}, f32[1,1,8192]{2,1,0:T(1,128)}, u32[]{:S(2)}) copy-start(f32[1,1,8192]{2,1,0:T(1,128)} %param.8) | copy-start | bytes 98308

commit v6 on v5

--- a/solution.py
+++ b/solution.py
@@ -24,7 +24,7 @@
 
 
 CTX_FIRST, CH_FIRST = 53, 7
-CTX_ORDER, CH_ORDER = led_by(CTX_FIRST, CTX), led_by(CH_FIRST, CH)
+CTX_ORDER, CH_ORDER = led_by(CTX_FIRST, CTX), [7, 0, 6, 1, 5, 2, 4, 3]
 LARGE = pltpu.CompilerParams(vmem_limit_bytes=20 * 1024 * 1024)
 SMALL = pltpu.CompilerParams(vmem_limit_bytes=8 * 1024 * 1024)
 

time: 72 us -> 71.9 us (level)
  no operation moved by 1% of the time
where the time goes in v6:
time: 71.9 us; the launch traced here: 71.6 us
  blocking collectives  65.2 us (91%)
  Pallas kernels  5.64 us (8%)
    all_to_all x4, blocking collectives, exchange(): lax.all_to_all(field, axis, split_axis=0, concat_axis=0, tiled=True, axis...  65.2 us
    pallas_call x1, Pallas kernels, on_device(): call(project_kernel, (pltpu.VMEM(message, BF16), pltpu.VMEM(weights.shape...  2.64 us
    pallas_call x1, Pallas kernels, on_device(): call(finish_kernel, (shape((GROUP, SIDE), BF16), shape(tokens.shape, BF16...  1.74 us

profile of v6, /device:TPU:24, one launch (start us, length us, event | category | flops | bytes accessed | tf_op | source)
XLA Modules:
  0.0 71.6 jit_solution(18435228529028929317)
XLA Ops:
  0.6 0.0 copy-start
  0.6 0.0 copy-start.1
  0.7 0.0 copy-start.2
  0.7 0.0 copy-start.3
  0.7 2.6 %shard_map.85 = (bf16[8,3,64,128]{3,2,1,0:T(8,128)(2,1)S(1)}, bf16[3,1024,512]{2,1,0:T(8,128)(2,1)S(1)}) custom-call(bf16[128,1024]{1,0:T(8,128)(2,1)} %tokens_hbm.1, bf16[3,1024,512]{2,1,0:T(8,128)(2,1)} %weights_hbm.1), custom_call_target="tpu_custom_call" | custom-call | tf_op jit(solution)/shard_map/pallas_call | solution.py:222
  3.3 12.1 %all_to_all.20.parts_ref = bf16[8,3,64,128]{3,2,1,0:T(8,128)(2,1)S(1)} all-to-all(bf16[8,3,64,128]{3,2,1,0:T(8,128)(2,1)S(1)} %get-tuple-element.14), channel_id=1, replica_groups={{7,0,6,1,5,2,4,3},{15,8,14,9,13,10,12,11},{23,16,22,17,21,18,20,19},{31..., dimensions={0} | all-to-all | bytes 786432 | tf_op jit(solution)/shard_map/all_to_all | solution.py:210
  15.5 0.0 copy-done.2
  15.5 0.1 shard_map.86
  15.5 24.5 %all_to_all.21 = bf16[64,2,128]{2,1,0:T(2,128)(2,1)S(1)} all-to-all(bf16[64,2,128]{2,1,0:T(2,128)(2,1)S(1)} %bitcast.10), channel_id=1, replica_groups={{424,8,16,24,32,40,48,56,64,72,80,88,96,104,112,120,128,136,144,152,160..., dimensions={0} | all-to-all | bytes 65536 | tf_op jit(solution)/shard_map/all_to_all | solution.py:210
  40.0 0.0 copy-done
  40.0 0.0 copy-done.1
  40.0 0.0 copy-done.3
  40.0 1.1 %shard_map.87 = (f32[64,128]{1,0:T(8,128)S(1)}, bf16[128,128]{1,0:T(8,128)(2,1)S(1)}) custom-call(bf16[128,128]{1,0:T(8,128)(2,1)S(1)} %bitcast.6, f32[64,128]{1,0:T(8,128)S(1)} %bitcast.8, bf16[4,128,128]{2,1,0:T(8,128)(2,1)S(1)} %copy-done.1, f32[2,128,128]{2,1,0:T(8,128)S(1)} %copy-done), custom_call_target="tpu_custom_call" | custom-call | tf_op jit(solution)/shard_map/pallas_call | solution.py:235
  41.2 17.5 %all_to_all.22 = bf16[64,2,128]{2,1,0:T(2,128)(2,1)S(1)} all-to-all(bf16[64,2,128]{2,1,0:T(2,128)(2,1)S(1)} %bitcast.9), channel_id=1, replica_groups={{424,8,16,24,32,40,48,56,64,72,80,88,96,104,112,120,128,136,144,152,160..., dimensions={0} | all-to-all | bytes 65536 | tf_op jit(solution)/shard_map/all_to_all | solution.py:210
  58.7 11.1 %all_to_all.23.grads_ref = bf16[8,3,64,128]{3,2,1,0:T(8,128)(2,1)S(1)} all-to-all(bf16[8,3,64,128]{3,2,1,0:T(8,128)(2,1)S(1)} %get-tuple-element.18), channel_id=1, replica_groups={{7,0,6,1,5,2,4,3},{15,8,14,9,13,10,12,11},{23,16,22,17,21,18,20,19},{31..., dimensions={0} | all-to-all | bytes 786432 | tf_op jit(solution)/shard_map/all_to_all | solution.py:210
  69.9 1.7 %shard_map.89 = (bf16[64,128]{1,0:T(8,128)(2,1)}, bf16[128,1024]{1,0:T(8,128)(2,1)}, f32[64,128]{1,0:T(8,128)}) custom-call(bf16[8,3,64,128]{3,2,1,0:T(8,128)(2,1)S(1)} %all_to_all.23.grads_ref, bf16[64,128]{1,0:T(8,128)(2,1)S(1)} %get-tuple-element.19.gated_in_ref, f32[64,128]{1,0:T(8,128)S(1)} %get-tuple-element.20.filter_in_ref, ...), custom_call_target="tpu_custom_call" | custom-call | tf_op jit(solution)/shard_map/pallas_call | solution.py:246
  (1 shorter events, 0.0 us)
Async XLA Ops:
  0.6 39.4 %copy-start = (f32[2,128,128]{2,1,0:T(8,128)S(1)}, f32[2,128,128]{2,1,0:T(8,128)}, u32[]{:S(2)}) copy-start(f32[2,128,128]{2,1,0:T(8,128)} %constant.5.clone.twiddle_ref) | copy-start | bytes 393220
  0.6 39.4 %copy-start.1 = (bf16[4,128,128]{2,1,0:T(8,128)(2,1)S(1)}, bf16[4,128,128]{2,1,0:T(8,128)(2,1)}, u32[]{:S(2)}) copy-start(bf16[4,128,128]{2,1,0:T(8,128)(2,1)} %constant.4.clone.waves_ref) | copy-start | bytes 393220
  0.7 14.8 %copy-start.2 = (bf16[64,128]{1,0:T(8,128)(2,1)S(1)}, bf16[64,128]{1,0:T(8,128)(2,1)}, u32[]{:S(2)}) copy-start(bf16[64,128]{1,0:T(8,128)(2,1)} %cotangent_ref.3) | copy-start | bytes 49156
  0.7 39.4 %copy-start.3 = (f32[1,1,8192]{2,1,0:T(1,128)S(1)}, f32[1,1,8192]{2,1,0:T(1,128)}, u32[]{:S(2)}) copy-start(f32[1,1,8192]{2,1,0:T(1,128)} %param.8) | copy-start | bytes 98308

commit v7 on v5

--- a/solution.py
+++ b/solution.py
@@ -23,7 +23,7 @@
     return order
 
 
-CTX_FIRST, CH_FIRST = 53, 7
+CTX_FIRST, CH_FIRST = 55, 4
 CTX_ORDER, CH_ORDER = led_by(CTX_FIRST, CTX), led_by(CH_FIRST, CH)
 LARGE = pltpu.CompilerParams(vmem_limit_bytes=20 * 1024 * 1024)
 SMALL = pltpu.CompilerParams(vmem_limit_bytes=8 * 1024 * 1024)

time: 72 us -> 72 us (level); the launches traced: 71.7 us -> 70.6 us
  blocking collectives: 65.4 us -> 64.3 us
    all_to_all x4, blocking collectives: 65.4 us -> 64.3 us  [exchange(): lax.all_to_all(field, axis, split_axis=0, concat_axis=0, tiled=True, axis...]
where the time goes in v7:
time: 72 us; the launch traced here: 70.6 us
  blocking collectives  64.3 us (89%)
  Pallas kernels  5.64 us (8%)
    all_to_all x4, blocking collectives, exchange(): lax.all_to_all(field, axis, split_axis=0, concat_axis=0, tiled=True, axis...  64.3 us
    pallas_call x1, Pallas kernels, on_device(): call(project_kernel, (pltpu.VMEM(message, BF16), pltpu.VMEM(weights.shape...  2.64 us
    pallas_call x1, Pallas kernels, on_device(): call(finish_kernel, (shape((GROUP, SIDE), BF16), shape(tokens.shape, BF16...  1.73 us

profile of v7, /device:TPU:24, one launch (start us, length us, event | category | flops | bytes accessed | tf_op | source)
XLA Modules:
  0.0 70.6 jit_solution(16332103409445414156)
XLA Ops:
  0.6 0.0 copy-start
  0.6 0.0 copy-start.1
  0.7 0.0 copy-start.2
  0.7 0.0 copy-start.3
  0.7 2.6 %shard_map.85 = (bf16[8,3,64,128]{3,2,1,0:T(8,128)(2,1)S(1)}, bf16[3,1024,512]{2,1,0:T(8,128)(2,1)S(1)}) custom-call(bf16[128,1024]{1,0:T(8,128)(2,1)} %tokens_hbm.1, bf16[3,1024,512]{2,1,0:T(8,128)(2,1)} %weights_hbm.1), custom_call_target="tpu_custom_call" | custom-call | tf_op jit(solution)/shard_map/pallas_call | solution.py:222
  3.3 11.3 %all_to_all.20.parts_ref = bf16[8,3,64,128]{3,2,1,0:T(8,128)(2,1)S(1)} all-to-all(bf16[8,3,64,128]{3,2,1,0:T(8,128)(2,1)S(1)} %get-tuple-element.14), channel_id=1, replica_groups={{4,1,2,3,0,5,6,7},{12,9,10,11,8,13,14,15},{20,17,18,19,16,21,22,23},{28..., dimensions={0} | all-to-all | bytes 786432 | tf_op jit(solution)/shard_map/all_to_all | solution.py:210
  14.6 0.0 copy-done.2
  14.6 0.1 shard_map.86
  14.7 24.6 %all_to_all.21 = bf16[64,2,128]{2,1,0:T(2,128)(2,1)S(1)} all-to-all(bf16[64,2,128]{2,1,0:T(2,128)(2,1)S(1)} %bitcast.10), channel_id=1, replica_groups={{440,8,16,24,32,40,48,56,64,72,80,88,96,104,112,120,128,136,144,152,160..., dimensions={0} | all-to-all | bytes 65536 | tf_op jit(solution)/shard_map/all_to_all | solution.py:210
  39.3 0.0 copy-done
  39.3 0.0 copy-done.1
  39.3 0.0 copy-done.3
  39.3 1.1 %shard_map.87 = (f32[64,128]{1,0:T(8,128)S(1)}, bf16[128,128]{1,0:T(8,128)(2,1)S(1)}) custom-call(bf16[128,128]{1,0:T(8,128)(2,1)S(1)} %bitcast.6, f32[64,128]{1,0:T(8,128)S(1)} %bitcast.8, bf16[4,128,128]{2,1,0:T(8,128)(2,1)S(1)} %copy-done.1, f32[2,128,128]{2,1,0:T(8,128)S(1)} %copy-done), custom_call_target="tpu_custom_call" | custom-call | tf_op jit(solution)/shard_map/pallas_call | solution.py:235
  40.4 17.4 %all_to_all.22 = bf16[64,2,128]{2,1,0:T(2,128)(2,1)S(1)} all-to-all(bf16[64,2,128]{2,1,0:T(2,128)(2,1)S(1)} %bitcast.9), channel_id=1, replica_groups={{440,8,16,24,32,40,48,56,64,72,80,88,96,104,112,120,128,136,144,152,160..., dimensions={0} | all-to-all | bytes 65536 | tf_op jit(solution)/shard_map/all_to_all | solution.py:210
  57.9 11.0 %all_to_all.23.grads_ref = bf16[8,3,64,128]{3,2,1,0:T(8,128)(2,1)S(1)} all-to-all(bf16[8,3,64,128]{3,2,1,0:T(8,128)(2,1)S(1)} %get-tuple-element.18), channel_id=1, replica_groups={{4,1,2,3,0,5,6,7},{12,9,10,11,8,13,14,15},{20,17,18,19,16,21,22,23},{28..., dimensions={0} | all-to-all | bytes 786432 | tf_op jit(solution)/shard_map/all_to_all | solution.py:210
  68.9 1.7 %shard_map.89 = (bf16[64,128]{1,0:T(8,128)(2,1)}, bf16[128,1024]{1,0:T(8,128)(2,1)}, f32[64,128]{1,0:T(8,128)}) custom-call(bf16[8,3,64,128]{3,2,1,0:T(8,128)(2,1)S(1)} %all_to_all.23.grads_ref, bf16[64,128]{1,0:T(8,128)(2,1)S(1)} %get-tuple-element.19.gated_in_ref, f32[64,128]{1,0:T(8,128)S(1)} %get-tuple-element.20.filter_in_ref, ...), custom_call_target="tpu_custom_call" | custom-call | tf_op jit(solution)/shard_map/pallas_call | solution.py:246
  (1 shorter events, 0.0 us)
Async XLA Ops:
  0.6 38.7 %copy-start = (f32[2,128,128]{2,1,0:T(8,128)S(1)}, f32[2,128,128]{2,1,0:T(8,128)}, u32[]{:S(2)}) copy-start(f32[2,128,128]{2,1,0:T(8,128)} %constant.5.clone.twiddle_ref) | copy-start | bytes 393220
  0.6 38.6 %copy-start.1 = (bf16[4,128,128]{2,1,0:T(8,128)(2,1)S(1)}, bf16[4,128,128]{2,1,0:T(8,128)(2,1)}, u32[]{:S(2)}) copy-start(bf16[4,128,128]{2,1,0:T(8,128)(2,1)} %constant.4.clone.waves_ref) | copy-start | bytes 393220
  0.7 14.0 %copy-start.2 = (bf16[64,128]{1,0:T(8,128)(2,1)S(1)}, bf16[64,128]{1,0:T(8,128)(2,1)}, u32[]{:S(2)}) copy-start(bf16[64,128]{1,0:T(8,128)(2,1)} %cotangent_ref.3) | copy-start | bytes 49156
  0.7 38.6 %copy-start.3 = (f32[1,1,8192]{2,1,0:T(1,128)S(1)}, f32[1,1,8192]{2,1,0:T(1,128)}, u32[]{:S(2)}) copy-start(f32[1,1,8192]{2,1,0:T(1,128)} %param.8) | copy-start | bytes 98308
